TPU v7x, 256 devices: a whole 4x4x8 slice. The times are simulated.
256 devices in a mesh: dp: 64 (over z, y, core), seq: 4 (over x).
Axes of the slice: x: 4, y: 4, z: 8, core: 2. Of those that a mesh axis runs over, the one named last changes fastest.
Arguments:
- queries: bfloat16 [32768, 3072], P(('dp', 'seq')), may hold values from -6 to 6
- keys: bfloat16 [32768, 3072], P(('dp', 'seq')), may hold values from -6 to 6
- values: bfloat16 [32768, 3072], P(('dp', 'seq')), may hold values from -6 to 6
- upstream: bfloat16 [32768, 3072], P(('dp', 'seq')), may hold values from -6 to 6
- dest_group: int32 [32768, 1], replicated, may hold values from 0 to 63; in each aligned block of 128 rows (0 to 127, 128 to 255, ...) at most 3 rows name the same one
- clip_ids: int32 [32768], replicated, may hold values from 0 to 2
Outputs:
- attended: bfloat16 [32768, 3072], P(('dp', 'seq'))
- grad_query: bfloat16 [32768, 3072], P(('dp', 'seq'))
- grad_key: bfloat16 [32768, 3072], P(('dp', 'seq'))
- grad_value: bfloat16 [32768, 3072], P(('dp', 'seq'))
Inputs may be any that keep to these rules, and one draw needn't show every extreme that they name: `dest_group`: among the rows of one device (aligned blocks of 128 rows) no data group is named more than 3 times; in every draw some device names some group exactly 3 times.
All inputs are finite; a program needn't handle non-finite values.
Results may differ from a plain program's by a relative error of at most 0.024.
Values may be sent and summed in bfloat16 or wider, within the bound.
No kernel may reach another device: no remote copies, remote signals or barrier semaphores. Data moves between devices by JAX's collectives and lax.ppermute only.
A program may use at most 128 MiB of HBM per device.

v0:
```python
import jax
import jax.numpy as jnp
from jax import lax
from jax.sharding import PartitionSpec as P

HD = 128


def prior_count(targets):
    length = targets.shape[-1]
    earlier = lax.broadcasted_iota(jnp.int32, (length, length), 1) < lax.broadcasted_iota(
        jnp.int32, (length, length), 0
    )
    matching = targets[..., :, None] == targets[..., None, :]
    return jnp.sum((matching & earlier).astype(jnp.int32), axis=-1)


def slot_labels(targets, clip_table, group_index, capacity):
    arriving = targets == group_index
    row_ranks = prior_count(targets)
    slot_ids = lax.broadcasted_iota(jnp.int32, (capacity,), 0)
    filled = arriving[:, None, :] & (row_ranks[:, None, :] == slot_ids[None, :, None])
    return jnp.sum(jnp.where(filled, clip_table[:, None, :] + 1, 0), axis=-1)


def select_rows(positions, slot_count, arrays):
    picker = (
        lax.broadcasted_iota(jnp.int32, (slot_count, positions.shape[0]), 0) == positions[None, :]
    ).astype(jnp.bfloat16)
    return tuple(
        (
            jnp.dot(picker, item, preferred_element_type=jnp.float32).astype(jnp.bfloat16)
            for item in arrays
        )
    )


def return_rows(positions, slot_count, stacked):
    picker = (
        positions[:, None] == lax.broadcasted_iota(jnp.int32, (positions.shape[0], slot_count), 1)
    ).astype(jnp.bfloat16)
    return jnp.einsum("ts,nsc->ntc", picker, stacked, preferred_element_type=jnp.float32).astype(
        jnp.bfloat16
    )


def attend_forward(query_rows, key_rows, value_rows, related):
    scale = HD ** (-0.5)
    contract_cols = (((1,), (1,)), ((), ()))
    prob_list, probs_b_list, out_list = ([], [], [])
    for head_index in range(query_rows.shape[1] // HD):
        lower = head_index * HD
        query_head = query_rows[:, lower : lower + HD]
        key_head = key_rows[:, lower : lower + HD]
        value_head = value_rows[:, lower : lower + HD]
        scores = (
            lax.dot_general(query_head, key_head, contract_cols, preferred_element_type=jnp.float32)
            * scale
        )
        scores = jnp.where(related, scores, -1e30)
        row_max = jnp.max(scores, axis=1, keepdims=True)
        weights = jnp.where(related, jnp.exp(scores - row_max), 0.0)
        probs = weights / jnp.sum(weights, axis=1, keepdims=True)
        probs_b = probs.astype(jnp.bfloat16)
        prob_list.append(probs)
        probs_b_list.append(probs_b)
        out_list.append(
            jnp.dot(probs_b, value_head, preferred_element_type=jnp.float32).astype(jnp.bfloat16)
        )
    return (prob_list, probs_b_list, jnp.concatenate(out_list, axis=1))


def attend_backward(
    query_rows, key_rows, value_rows, upstream_rows, attended, prob_list, probs_b_list
):
    scale = HD ** (-0.5)
    contract_cols = (((1,), (1,)), ((), ()))
    contract_rows = (((0,), (0,)), ((), ()))
    query_grads, key_grads, value_grads = ([], [], [])
    for head_index in range(query_rows.shape[1] // HD):
        lower = head_index * HD
        query_head = query_rows[:, lower : lower + HD]
        key_head = key_rows[:, lower : lower + HD]
        value_head = value_rows[:, lower : lower + HD]
        upstream_head = upstream_rows[:, lower : lower + HD]
        out_head = attended[:, lower : lower + HD]
        delta = jnp.sum(
            upstream_head.astype(jnp.float32) * out_head.astype(jnp.float32), axis=1, keepdims=True
        )
        dprobs = lax.dot_general(
            upstream_head, value_head, contract_cols, preferred_element_type=jnp.float32
        )
        dscores = (prob_list[head_index] * (dprobs - delta)).astype(jnp.bfloat16)
        query_grads.append(
            (jnp.dot(dscores, key_head, preferred_element_type=jnp.float32) * scale).astype(
                jnp.bfloat16
            )
        )
        key_grads.append(
            (
                lax.dot_general(
                    dscores, query_head, contract_rows, preferred_element_type=jnp.float32
                )
                * scale
            ).astype(jnp.bfloat16)
        )
        value_grads.append(
            lax.dot_general(
                probs_b_list[head_index],
                upstream_head,
                contract_rows,
                preferred_element_type=jnp.float32,
            ).astype(jnp.bfloat16)
        )
    return (
        jnp.concatenate(query_grads, axis=1),
        jnp.concatenate(key_grads, axis=1),
        jnp.concatenate(value_grads, axis=1),
    )


def body(queries, keys, values, upstream, dest_group, clip_ids):
    group_count = lax.axis_size("dp")
    part_count = lax.axis_size("seq")
    group_index = lax.axis_index("dp")
    seq_index = lax.axis_index("seq")
    row_count = queries.shape[0]
    capacity = (3 * row_count + 2 * group_count - 1) // (2 * group_count)
    targets = dest_group[:, 0].reshape(group_count, part_count, row_count)
    clip_table = clip_ids.reshape(group_count, part_count, row_count)
    label_table = slot_labels(
        targets.reshape(group_count * part_count, row_count),
        clip_table.reshape(group_count * part_count, row_count),
        group_index,
        capacity,
    ).reshape(group_count, part_count, capacity)
    own_group = lax.dynamic_index_in_dim(targets, group_index, 0, keepdims=False)
    labels = jnp.transpose(label_table, (1, 0, 2)).reshape(-1)
    own_rows = lax.dynamic_index_in_dim(own_group, seq_index, 0, keepdims=False)
    positions = own_rows * capacity + prior_count(own_rows)
    packed = select_rows(positions, group_count * capacity, (queries, keys, values, upstream))
    routed = (
        lax.all_to_all(packed[0], "dp", split_axis=0, concat_axis=0, tiled=True),
        lax.all_to_all(packed[1], "dp", split_axis=0, concat_axis=0, tiled=True),
        lax.all_to_all(packed[2], "dp", split_axis=0, concat_axis=0, tiled=True),
        lax.all_to_all(packed[3], "dp", split_axis=0, concat_axis=0, tiled=True),
    )
    regrouped = (
        lax.all_to_all(routed[0], "seq", split_axis=1, concat_axis=0, tiled=True),
        lax.all_to_all(routed[1], "seq", split_axis=1, concat_axis=0, tiled=True),
        lax.all_to_all(routed[2], "seq", split_axis=1, concat_axis=0, tiled=True),
        lax.all_to_all(routed[3], "seq", split_axis=1, concat_axis=0, tiled=True),
    )
    slot_total = labels.shape[0]
    identity = lax.broadcasted_iota(jnp.int32, (slot_total, slot_total), 0) == lax.broadcasted_iota(
        jnp.int32, (slot_total, slot_total), 1
    )
    related = (labels[:, None] == labels[None, :]) & (labels[:, None] > 0) | identity
    prob_list, probs_b_list, attended = attend_forward(
        regrouped[0], regrouped[1], regrouped[2], related
    )
    gradients = attend_backward(
        regrouped[0], regrouped[1], regrouped[2], regrouped[3], attended, prob_list, probs_b_list
    )
    heads_back = lax.all_to_all(
        jnp.stack((attended, gradients[0], gradients[1], gradients[2])),
        "seq",
        split_axis=1,
        concat_axis=2,
        tiled=True,
    )
    routed_back = lax.all_to_all(heads_back, "dp", split_axis=1, concat_axis=1, tiled=True)
    all_home = return_rows(positions, group_count * capacity, routed_back)
    return (all_home[0], all_home[1], all_home[2], all_home[3])


def solution(mesh):
    return jax.shard_map(
        body,
        mesh=mesh,
        in_specs=(
            P(("dp", "seq"), None),
            P(("dp", "seq"), None),
            P(("dp", "seq"), None),
            P(("dp", "seq"), None),
            P(),
            P(),
        ),
        out_specs=(
            P(("dp", "seq"), None),
            P(("dp", "seq"), None),
            P(("dp", "seq"), None),
            P(("dp", "seq"), None),
        ),
        check_vma=False,
    )
```

profile of v0, /device:TPU:1, one launch (start us, length us, event | category | flops | bytes accessed | tf_op | source)
XLA Modules:
  0.0 560.0 jit_solution(12021356061418666371)
XLA Ops:
  4.9 13.2 %all-to-all-start.6 = ((bf16[64,3,3072]{2,1,0:T(4,128)(2,1)}), bf16[64,3,3072]{2,1,0:T(4,128)(2,1)S(1)}, u32[]{:S(2)}, u32[]{:S(2)}) async-start(bf16[64,3,3072]{2,1,0:T(4,128)(2,1)} %all_to_all.114), calls=%async_computation.6 | async-start | bytes 3145728 | tf_op jit(solution)/shard_map/all_to_all | solution.py:146
  20.6 36.4 %all-to-all-done.6 = bf16[64,3,3072]{2,1,0:T(4,128)(2,1)S(1)} async-done(((bf16[64,3,3072]{2,1,0:T(4,128)(2,1)}), bf16[64,3,3072]{2,1,0:T(4,128)(2,1)S(1)}, u32[]{:S(2)}, u32[]{:S(2)}) %all-to-all-start.6) | async-done | bytes 1179680 | tf_op jit(solution)/shard_map/all_to_all | solution.py:146
  57.0 6.6 %all-to-all-start.2 = ((bf16[64,3,3072]{2,1,0:T(4,128)(2,1)}), bf16[64,3,3072]{2,1,0:T(4,128)(2,1)}, u32[]{:S(2)}, u32[]{:S(2)}) async-start(bf16[64,3,3072]{2,1,0:T(4,128)(2,1)} %all_to_all.102), calls=%async_computation.2 | async-start | bytes 3145728 | tf_op jit(solution)/shard_map/all_to_all | solution.py:144
  66.2 36.4 %all-to-all-done.2 = bf16[64,3,3072]{2,1,0:T(4,128)(2,1)} async-done(((bf16[64,3,3072]{2,1,0:T(4,128)(2,1)}), bf16[64,3,3072]{2,1,0:T(4,128)(2,1)}, u32[]{:S(2)}, u32[]{:S(2)}) %all-to-all-start.2) | async-done | bytes 1179680 | tf_op jit(solution)/shard_map/all_to_all | solution.py:144
  102.6 6.6 %all-to-all-start = ((bf16[64,3,3072]{2,1,0:T(4,128)(2,1)}), bf16[64,3,3072]{2,1,0:T(4,128)(2,1)}, u32[]{:S(2)}, u32[]{:S(2)}) async-start(bf16[64,3,3072]{2,1,0:T(4,128)(2,1)} %all_to_all.96), calls=%async_computation | async-start | bytes 3145728 | tf_op jit(solution)/shard_map/all_to_all | solution.py:143
  111.8 36.4 %all-to-all-done = bf16[64,3,3072]{2,1,0:T(4,128)(2,1)} async-done(((bf16[64,3,3072]{2,1,0:T(4,128)(2,1)}), bf16[64,3,3072]{2,1,0:T(4,128)(2,1)}, u32[]{:S(2)}, u32[]{:S(2)}) %all-to-all-start) | async-done | bytes 1179680 | tf_op jit(solution)/shard_map/all_to_all | solution.py:143
  148.2 6.6 %all-to-all-start.4 = ((bf16[64,3,3072]{2,1,0:T(4,128)(2,1)}), bf16[64,3,3072]{2,1,0:T(4,128)(2,1)}, u32[]{:S(2)}, u32[]{:S(2)}) async-start(bf16[64,3,3072]{2,1,0:T(4,128)(2,1)} %all_to_all.108), calls=%async_computation.4 | async-start | bytes 3145728 | tf_op jit(solution)/shard_map/all_to_all | solution.py:145
  154.8 2.8 all_to_all.104
  158.8 34.9 %all-to-all-done.4 = bf16[64,3,3072]{2,1,0:T(4,128)(2,1)} async-done(((bf16[64,3,3072]{2,1,0:T(4,128)(2,1)}), bf16[64,3,3072]{2,1,0:T(4,128)(2,1)}, u32[]{:S(2)}, u32[]{:S(2)}) %all-to-all-start.4) | async-done | bytes 1179680 | tf_op jit(solution)/shard_map/all_to_all | solution.py:145
  193.7 4.3 all-to-all-start.3
  198.1 2.8 all_to_all.98
  202.0 10.9 %all-to-all-done.3 = bf16[192,4,768]{2,0,1:T(8,128)(2,1)} async-done(((bf16[192,4,768]{2,0,1:T(8,128)(2,1)}), bf16[192,4,768]{2,0,1:T(8,128)(2,1)}, u32[]{:S(2)}, u32[]{:S(2)}) %all-to-all-start.3) | async-done | bytes 1179680 | tf_op jit(solution)/shard_map/all_to_all | solution.py:150
  212.9 3.5 all-to-all-start.1
  216.5 10.3 %convert_reduce_fusion = s32[256,128]{1,0:T(8,128)S(1)} fusion(s32[256,128]{1,0:T(8,128)S(1)} %bitcast.79, pred[128,128]{1,0:T(8,128)(4,1)S(1)} %iota_compare_fusion.8), kind=kLoop, calls=%fused_computation | loop fusion | flops 16744448 | bytes 278528 | tf_op jit(solution)/shard_map/reduce_sum | solution.py:15
  227.9 2.2 all_to_all.116
  230.1 2.4 copy.120
  232.6 2.8 all_to_all.110
  236.5 4.7 all-to-all-start.7
  242.7 3.1 fusion.94
  245.7 2.8 fusion.87
  250.0 3.3 fusion.14
  254.4 4.3 all-to-all-start.5
  258.7 9.2 %fusion.26 = (f32[768]{0:T(1024)}, f32[768]{0:T(1024)}, f32[768]{0:T(1024)}, f32[768]{0:T(1024)}, f32[768]{0:T(1024)S(1)}, /*index=5*/f32[768]{0:T(1024)S(1)}, f32[768,768]{0,1:T(8,128)}) fusion(f32[768,768]{0,1:T(8,128)} %get-tuple-element.50, f32[768]{0:T(1024)S(1)} %get-tuple-element.34, pred[768]{0:T(1024)(128)(4,1)S(1)} %broadcast_compare_fusion.1, ...), kind=kOutput, calls=%fused_computation.47 | convolution fusion | flops 166325760 | bytes 14584832 | tf_op jit(solution)/shard_map/dot_general | solution.py:57
  270.2 3.6 fusion.56
  273.8 3.1 multiply_reduce_fusion.5
  276.9 2.3 multiply_convert_fusion.5
  279.2 2.2 fusion.40
  284.2 6.1 %fusion.24 = (f32[768]{0:T(1024)}, f32[768]{0:T(1024)S(1)}, f32[768]{0:T(1024)}, f32[768]{0:T(1024)}) fusion(f32[768,768]{0,1:T(8,128)S(1)} %fusion.80, f32[768]{0:T(1024)S(1)} %get-tuple-element.33, pred[768]{0:T(1024)(128)(4,1)} %copy-done.30, s32[768]{0:T(1024)S(1)} %eq.91, f32[768]{0:T(1024)} %get-tuple-element.30, f32[768,768]{0,1:T(8,128)} %get-tuple-element.51, ...), kind=kLoop, calls=%fused_computation.45 | loop fusion | flops 14152704 | bytes 9465600 | tf_op jit(solution)/shard_map/reduce_sum | solution.py:63
  290.4 2.9 fusion.55
  295.4 3.3 multiply_convert_fusion.4
  299.5 3.7 fusion.54
  303.3 2.1 multiply_reduce_fusion.3
  305.5 3.3 multiply_convert_fusion.3
  309.6 3.7 fusion.53
  313.4 2.1 multiply_reduce_fusion.2
  315.5 3.3 multiply_convert_fusion.2
  319.7 3.1 fusion.52
  324.9 3.3 multiply_convert_fusion.1
  328.4 3.7 fusion.51
  332.1 2.1 multiply_reduce_fusion
  334.3 2.4 multiply_convert_fusion
  346.6 2.5 pad_maximum_fusion
  349.1 8.6 %copy.133 = bf16[4,768,768]{2,0,1:T(4,128)(2,1)} copy(bf16[4,768,768]{1,2,0:T(8,128)(2,1)} %pad_maximum_fusion) | data formatting | bytes 9437184 | tf_op jit(solution)/shard_map/stack | solution.py:166
  357.7 53.7 %all_to_all.135 = bf16[4,768,768]{2,0,1:T(4,128)(2,1)S(1)} all-to-all(bf16[4,768,768]{2,0,1:T(4,128)(2,1)} %copy.133), channel_id=1, replica_groups=mesh['dp'=64,'seq'=4] {'seq'}, dimensions={1} | all-to-all | bytes 9437184 | tf_op jit(solution)/shard_map/all_to_all | solution.py:165
  412.0 5.8 %copy.148 = bf16[4,192,4,768]{3,2,0,1:T(4,128)(2,1)} copy(bf16[4,192,4,768]{3,1,2,0:T(8,128)(2,1)S(1)} %bitcast.61) | data formatting | bytes 9437184 | tf_op jit(solution)/shard_map/all_to_all | solution.py:165
  417.8 10.0 %reshape.109 = bf16[4,192,3072]{2,0,1:T(4,128)(2,1)} reshape(bf16[4,192,4,768]{3,2,0,1:T(4,128)(2,1)} %copy.148) | data formatting | bytes 9437184 | tf_op jit(solution)/shard_map/all_to_all | solution.py:165
  427.8 123.1 %all_to_all.136 = bf16[4,192,3072]{2,0,1:T(4,128)(2,1)S(1)} all-to-all(bf16[4,192,3072]{2,0,1:T(4,128)(2,1)} %reshape.109), channel_id=1, replica_groups=mesh['dp'=64,'seq'=4] {'dp'}, dimensions={1} | all-to-all | bytes 9437184 | tf_op jit(solution)/shard_map/all_to_all | solution.py:172
  550.9 3.9 fusion.5
  (145 shorter events, 47.6 us)
Async XLA Ops:
  2.8 15.3 %copy-start.17 = (bf16[128,3072]{1,0:T(8,128)(2,1)S(1)}, bf16[128,3072]{1,0:T(8,128)(2,1)}, u32[]{:S(2)}) copy-start(bf16[128,3072]{1,0:T(8,128)(2,1)} %param.7) | copy-start | bytes 2359300
  4.9 52.2 %all-to-all-start.6 = ((bf16[64,3,3072]{2,1,0:T(4,128)(2,1)}), bf16[64,3,3072]{2,1,0:T(4,128)(2,1)S(1)}, u32[]{:S(2)}, u32[]{:S(2)}) async-start(bf16[64,3,3072]{2,1,0:T(4,128)(2,1)} %all_to_all.114), calls=%async_computation.6 | async-start | bytes 3145728 | tf_op jit(solution)/shard_map/all_to_all | solution.py:146
  18.5 45.2 %copy-start.18 = (bf16[128,3072]{1,0:T(8,128)(2,1)S(1)}, bf16[128,3072]{1,0:T(8,128)(2,1)}, u32[]{:S(2)}) copy-start(bf16[128,3072]{1,0:T(8,128)(2,1)} %param.6) | copy-start | bytes 2359300
  57.0 45.6 %all-to-all-start.2 = ((bf16[64,3,3072]{2,1,0:T(4,128)(2,1)}), bf16[64,3,3072]{2,1,0:T(4,128)(2,1)}, u32[]{:S(2)}, u32[]{:S(2)}) async-start(bf16[64,3,3072]{2,1,0:T(4,128)(2,1)} %all_to_all.102), calls=%async_computation.2 | async-start | bytes 3145728 | tf_op jit(solution)/shard_map/all_to_all | solution.py:144
  64.1 45.1 %copy-start.19 = (bf16[128,3072]{1,0:T(8,128)(2,1)S(1)}, bf16[128,3072]{1,0:T(8,128)(2,1)}, u32[]{:S(2)}) copy-start(bf16[128,3072]{1,0:T(8,128)(2,1)} %param.8) | copy-start | bytes 2359300
  102.6 45.6 %all-to-all-start = ((bf16[64,3,3072]{2,1,0:T(4,128)(2,1)}), bf16[64,3,3072]{2,1,0:T(4,128)(2,1)}, u32[]{:S(2)}, u32[]{:S(2)}) async-start(bf16[64,3,3072]{2,1,0:T(4,128)(2,1)} %all_to_all.96), calls=%async_computation | async-start | bytes 3145728 | tf_op jit(solution)/shard_map/all_to_all | solution.py:143
  148.2 45.6 %all-to-all-start.4 = ((bf16[64,3,3072]{2,1,0:T(4,128)(2,1)}), bf16[64,3,3072]{2,1,0:T(4,128)(2,1)}, u32[]{:S(2)}, u32[]{:S(2)}) async-start(bf16[64,3,3072]{2,1,0:T(4,128)(2,1)} %all_to_all.108), calls=%async_computation.4 | async-start | bytes 3145728 | tf_op jit(solution)/shard_map/all_to_all | solution.py:145
  157.6 40.4 %copy-start.10 = (s32[32768,1]{0,1:T(1,128)S(1)}, s32[32768,1]{0,1:T(1,128)}, u32[]{:S(2)}) copy-start(s32[32768,1]{0,1:T(1,128)} %param.10) | copy-start | bytes 393220
  157.6 40.4 %copy-start.24 = (s32[32768]{0:T(1024)S(1)}, s32[32768]{0:T(1024)}, u32[]{:S(2)}) copy-start(s32[32768]{0:T(1024)} %param.11) | copy-start | bytes 393220
  193.7 19.2 %all-to-all-start.3 = ((bf16[192,4,768]{2,0,1:T(8,128)(2,1)}), bf16[192,4,768]{2,0,1:T(8,128)(2,1)}, u32[]{:S(2)}, u32[]{:S(2)}) async-start(bf16[192,4,768]{2,0,1:T(8,128)(2,1)} %copy.118), calls=%async_computation.3 | async-start | bytes 2359296 | tf_op jit(solution)/shard_map/all_to_all | solution.py:150
  212.9 23.6 %all-to-all-start.1 = ((bf16[192,4,768]{2,0,1:T(8,128)(2,1)}), bf16[192,4,768]{2,0,1:T(8,128)(2,1)S(1)}, u32[]{:S(2)}, u32[]{:S(2)}) async-start(bf16[192,4,768]{2,0,1:T(8,128)(2,1)} %copy.117), calls=%async_computation.1 | async-start | bytes 2359296 | tf_op jit(solution)/shard_map/all_to_all | solution.py:149
  227.9 30.8 %copy-start.30 = (pred[768]{0:T(1024)(128)(4,1)}, pred[768]{0:T(1024)(128)(4,1)S(1)}, u32[]{:S(2)}) copy-start(pred[768]{0:T(1024)(128)(4,1)S(1)} %broadcast_compare_fusion.1) | copy-start | bytes 2308
  236.5 9.2 %copy-start.4 = (bf16[192,4,768]{2,0,1:T(8,128)(2,1)}, bf16[192,4,768]{2,0,1:T(8,128)(2,1)S(1)}, u32[]{:S(2)}) copy-start(bf16[192,4,768]{2,0,1:T(8,128)(2,1)S(1)} %all-to-all-done.1) | copy-start | bytes 3538948
  236.5 17.9 %all-to-all-start.7 = ((bf16[192,4,768]{2,0,1:T(8,128)(2,1)}), bf16[192,4,768]{2,0,1:T(8,128)(2,1)}, u32[]{:S(2)}, u32[]{:S(2)}) async-start(bf16[192,4,768]{2,0,1:T(8,128)(2,1)} %copy.120), calls=%async_computation.7 | async-start | bytes 2359296 | tf_op jit(solution)/shard_map/all_to_all | solution.py:152
  242.7 7.4 %copy-start.6 = (f32[768,768]{0,1:T(8,128)}, f32[768,768]{0,1:T(8,128)S(1)}, u32[]{:S(2)}) copy-start(f32[768,768]{0,1:T(8,128)S(1)} %fusion.108) | copy-start | bytes 7077892
  253.4 14.5 %copy-start.37 = (f32[768]{0:T(1024)}, f32[768]{0:T(1024)S(1)}, u32[]{:S(2)}) copy-start(f32[768]{0:T(1024)S(1)} %get-tuple-element.34) | copy-start | bytes 9220
  253.4 14.5 %copy-start.39 = (f32[768]{0:T(1024)}, f32[768]{0:T(1024)S(1)}, u32[]{:S(2)}) copy-start(f32[768]{0:T(1024)S(1)} %get-tuple-element.35) | copy-start | bytes 9220
  254.4 19.3 %all-to-all-start.5 = ((bf16[192,4,768]{2,0,1:T(8,128)(2,1)}), bf16[192,4,768]{2,0,1:T(8,128)(2,1)}, u32[]{:S(2)}, u32[]{:S(2)}) async-start(bf16[192,4,768]{2,0,1:T(8,128)(2,1)} %copy.119), calls=%async_computation.5 | async-start | bytes 2359296 | tf_op jit(solution)/shard_map/all_to_all | solution.py:151
  273.8 3.1 copy-start.7
  273.8 3.1 copy-start.31
  273.8 3.1 copy-start.40
  273.8 3.1 copy-start.42
  284.2 6.1 %copy-start.8 = (f32[768,768]{0,1:T(8,128)S(1)}, f32[768,768]{0,1:T(8,128)}, u32[]{:S(2)}) copy-start(f32[768,768]{0,1:T(8,128)} %get-tuple-element.51) | copy-start | bytes 7077892
  284.2 6.1 %copy-start.27 = (f32[768]{0:T(1024)S(1)}, f32[768]{0:T(1024)}, u32[]{:S(2)}) copy-start(f32[768]{0:T(1024)} %get-tuple-element.30) | copy-start | bytes 9220
  284.2 6.1 %copy-start.32 = (pred[768]{0:T(1024)(128)(4,1)S(1)}, pred[768]{0:T(1024)(128)(4,1)}, u32[]{:S(2)}) copy-start(pred[768]{0:T(1024)(128)(4,1)} %copy-done.30) | copy-start | bytes 2308
  290.4 2.9 copy-start.20
  299.5 3.8 copy-start.3
  299.5 3.8 copy-start.22
  299.5 3.8 copy-start.25
  299.5 3.8 copy-start.29
  299.5 3.8 copy-start.33
  309.6 3.7 copy-start.2
  309.6 3.7 copy-start.23
  309.6 3.8 copy-start.28
  309.6 3.8 copy-start.34
  319.6 3.1 copy-start.21
  319.6 3.1 copy-start.26
  319.6 3.1 copy-start.35
  328.4 3.8 copy-start.36
  328.4 3.8 copy-start.38
  328.4 3.8 copy-start.41
  334.3 2.5 copy-start.5
  334.3 2.5 copy-start.9
  334.3 2.5 copy-start.13
  334.3 3.0 copy-start.11
  337.4 3.4 copy-start.15
  339.3 3.3 copy-start.16
  556.1 3.5 copy-start.1
  (3 other events, 5.2 us)
where the time goes:
time: 569 us; the launch traced here: 560 us
  blocking collectives  177 us (31%)
  waiting for transfers between devices  156 us (27%)
  matrix products  93.1 us (16%)
  local copies, waits for them, and re-layouts  62.3 us (11%)
  starting transfers between devices  49.8 us (9%)
  other arithmetic  20 us (4%)
    all_to_all x1, blocking collectives, body(): lax.all_to_all(heads_back, 'dp', split_axis=1, concat_axis=1, tiled=True)  123 us
    all_to_all x1, blocking collectives, body(): lax.all_to_all(jnp.stack((attended, gradients[0], gradients[1], gradients...  53.7 us
    all_to_all x1, waiting for transfers between devices, body(): lax.all_to_all(packed[3], 'dp', split_axis=0, concat_axis=0, tiled=True)  36.4 us
    all_to_all x1, waiting for transfers between devices, body(): lax.all_to_all(packed[1], 'dp', split_axis=0, concat_axis=0, tiled=True)  36.4 us
    all_to_all x1, waiting for transfers between devices, body(): lax.all_to_all(packed[0], 'dp', split_axis=0, concat_axis=0, tiled=True)  36.4 us
    all_to_all x1, waiting for transfers between devices, body(): lax.all_to_all(packed[2], 'dp', split_axis=0, concat_axis=0, tiled=True)  34.9 us
    dot_general x6, matrix products, attend_forward(): lax.dot_general(query_head, key_head, contract_cols, preferred_element_ty...  21.2 us
    dot_general x6, matrix products, attend_backward(): lax.dot_general(probs_b_list[head_index], upstream_head, contract_rows, p...  20.8 us
  transfers between devices with their start and end apart: 8, of which 6 were waited for; matrix products, arithmetic and copies ran while one was open for 8% of the time, Pallas kernels for 0%

commit v1 on v0

--- a/solution.py
+++ b/solution.py
@@ -21,18 +21,6 @@
     slot_ids = lax.broadcasted_iota(jnp.int32, (capacity,), 0)
     filled = arriving[:, None, :] & (row_ranks[:, None, :] == slot_ids[None, :, None])
     return jnp.sum(jnp.where(filled, clip_table[:, None, :] + 1, 0), axis=-1)
-
-
-def select_rows(positions, slot_count, arrays):
-    picker = (
-        lax.broadcasted_iota(jnp.int32, (slot_count, positions.shape[0]), 0) == positions[None, :]
-    ).astype(jnp.bfloat16)
-    return tuple(
-        (
-            jnp.dot(picker, item, preferred_element_type=jnp.float32).astype(jnp.bfloat16)
-            for item in arrays
-        )
-    )
 
 
 def return_rows(positions, slot_count, stacked):
@@ -135,22 +123,22 @@
         capacity,
     ).reshape(group_count, part_count, capacity)
     own_group = lax.dynamic_index_in_dim(targets, group_index, 0, keepdims=False)
-    labels = jnp.transpose(label_table, (1, 0, 2)).reshape(-1)
+    labels = label_table.reshape(-1)
     own_rows = lax.dynamic_index_in_dim(own_group, seq_index, 0, keepdims=False)
     positions = own_rows * capacity + prior_count(own_rows)
-    packed = select_rows(positions, group_count * capacity, (queries, keys, values, upstream))
-    routed = (
-        lax.all_to_all(packed[0], "dp", split_axis=0, concat_axis=0, tiled=True),
-        lax.all_to_all(packed[1], "dp", split_axis=0, concat_axis=0, tiled=True),
-        lax.all_to_all(packed[2], "dp", split_axis=0, concat_axis=0, tiled=True),
-        lax.all_to_all(packed[3], "dp", split_axis=0, concat_axis=0, tiled=True),
+    slots = group_count * capacity
+    picker = (
+        lax.broadcasted_iota(jnp.int32, (slots, row_count), 0) == positions[None, :]
+    ).astype(jnp.bfloat16)
+    width = queries.shape[1] // part_count
+    stacked = jnp.stack((queries, keys, values, upstream))
+    packed = jnp.einsum("st,ntc->snc", picker, stacked, preferred_element_type=jnp.float32).astype(
+        jnp.bfloat16
     )
-    regrouped = (
-        lax.all_to_all(routed[0], "seq", split_axis=1, concat_axis=0, tiled=True),
-        lax.all_to_all(routed[1], "seq", split_axis=1, concat_axis=0, tiled=True),
-        lax.all_to_all(routed[2], "seq", split_axis=1, concat_axis=0, tiled=True),
-        lax.all_to_all(routed[3], "seq", split_axis=1, concat_axis=0, tiled=True),
-    )
+    blocks = packed.reshape(group_count, capacity, 4, part_count, width)
+    blocks = jnp.transpose(blocks, (0, 3, 1, 2, 4)).reshape(-1, capacity, 4, width)
+    arrived = lax.all_to_all(blocks, ("dp", "seq"), split_axis=0, concat_axis=0, tiled=True)
+    regrouped = jnp.transpose(arrived, (2, 0, 1, 3)).reshape(4, -1, width)
     slot_total = labels.shape[0]
     identity = lax.broadcasted_iota(jnp.int32, (slot_total, slot_total), 0) == lax.broadcasted_iota(
         jnp.int32, (slot_total, slot_total), 1
@@ -162,15 +150,12 @@
     gradients = attend_backward(
         regrouped[0], regrouped[1], regrouped[2], regrouped[3], attended, prob_list, probs_b_list
     )
-    heads_back = lax.all_to_all(
-        jnp.stack((attended, gradients[0], gradients[1], gradients[2])),
-        "seq",
-        split_axis=1,
-        concat_axis=2,
-        tiled=True,
-    )
-    routed_back = lax.all_to_all(heads_back, "dp", split_axis=1, concat_axis=1, tiled=True)
-    all_home = return_rows(positions, group_count * capacity, routed_back)
+    results = jnp.stack((attended, gradients[0], gradients[1], gradients[2]), axis=1)
+    results = results.reshape(-1, capacity, 4, width)
+    routed_back = lax.all_to_all(results, ("dp", "seq"), split_axis=0, concat_axis=0, tiled=True)
+    routed_back = routed_back.reshape(group_count, part_count, capacity, 4, width)
+    routed_back = jnp.transpose(routed_back, (3, 0, 2, 1, 4)).reshape(4, slots, -1)
+    all_home = return_rows(positions, slots, routed_back)
     return (all_home[0], all_home[1], all_home[2], all_home[3])
 
 

time: 569 us -> 485 us (0.85)
  local copies, waits for them, and re-layouts: 62.3 us -> 130 us
  blocking collectives: 177 us -> 116 us
  waiting for transfers between devices: 156 us -> 97.6 us
  starting transfers between devices: 49.8 us -> 16.9 us
    all_to_all x2 -> x1, blocking collectives: 177 us -> 116 us  [body(): lax.all_to_all(results, ('dp', 'seq'), split_axis=0, concat_axis=0, tiled...]
    all_to_all x8 -> x1, waiting for transfers between devices: 156 us -> 97.6 us  [body(): lax.all_to_all(blocks, ('dp', 'seq'), split_axis=0, concat_axis=0, tiled=...]
    all_to_all x15 -> x0, local copies, waits for them, and re-layouts: 41.2 us -> none  [the longest x3 16.4 us: body(): lax.all_to_all(jnp.stack((attended, gradients[0], gradients[1], gradients...]
    slice x0 -> x1, local copies, waits for them, and re-layouts: none -> 35.7 us  [body(): regrouped[2]]
    reshape x1 -> x4, local copies, waits for them, and re-layouts: 0.12 us -> 33.6 us  [the longest x2 20.3 us: body(): blocks = packed.reshape(group_count, capacity, 4, part_count, width)]
    all_to_all x8 -> x1, starting transfers between devices: 49.8 us -> 16.9 us  [body(): lax.all_to_all(blocks, ('dp', 'seq'), split_axis=0, concat_axis=0, tiled=...]
    unnamed x102 -> x136, local copies, waits for them, and re-layouts: 10.6 us -> 23 us
    squeeze x0 -> x4, local copies, waits for them, and re-layouts: none -> 11.3 us  [the longest x1 3.97 us: body(): regrouped[2]]
  transfers between devices with their start and end apart: 8 -> 1, of which waited for: 6 -> 1; matrix products, arithmetic and copies ran while one was open for 8% -> 2% of each run, Pallas kernels for 0% -> 0%
where the time goes in v1:
time: 485 us; the launch traced here: 476 us
  local copies, waits for them, and re-layouts  130 us (27%)
  blocking collectives  116 us (24%)
  waiting for transfers between devices  97.6 us (20%)
  matrix products  91.9 us (19%)
  other arithmetic  22.2 us (5%)
  starting transfers between devices  16.9 us (3%)
    all_to_all x1, blocking collectives, body(): lax.all_to_all(results, ('dp', 'seq'), split_axis=0, concat_axis=0, tiled...  116 us
    all_to_all x1, waiting for transfers between devices, body(): lax.all_to_all(blocks, ('dp', 'seq'), split_axis=0, concat_axis=0, tiled=...  97.6 us
    slice x1, local copies, waits for them, and re-layouts, body(): regrouped[2]  35.7 us
    unnamed x136, local copies, waits for them, and re-layouts  23 us
    dot_general x6, matrix products, attend_forward(): jnp.dot(probs_b, value_head, preferred_element_type=jnp.float32)  21.5 us
    reshape x2, local copies, waits for them, and re-layouts, body(): blocks = packed.reshape(group_count, capacity, 4, part_count, width)  20.3 us
    dot_general x6, matrix products, attend_backward(): lax.dot_general(upstream_head, value_head, contract_cols, preferred_eleme...  18.2 us
    all_to_all x1, starting transfers between devices, body(): lax.all_to_all(blocks, ('dp', 'seq'), split_axis=0, concat_axis=0, tiled=...  16.9 us
  transfers between devices with their start and end apart: 1, of which 1 were waited for; matrix products, arithmetic and copies ran while one was open for 2% of the time, Pallas kernels for 0%

profile of v1, /device:TPU:1, one launch (start us, length us, event | category | flops | bytes accessed | tf_op | source)
XLA Modules:
  0.0 476.2 jit_solution(4077049925288180453)
XLA Ops:
  2.7 5.4 %convolution_convert_fusion = bf16[192,4,3072]{2,0,1:T(8,128)(2,1)} fusion(bf16[1,128,3072]{2,1,0:T(8,128)(2,1)} %bitcast.58, bf16[1,128,3072]{2,1,0:T(8,128)(2,1)} %bitcast.59, bf16[1,128,3072]{2,1,0:T(8,128)(2,1)} %bitcast.60, bf16[1,128,3072]{2,1,0:T(8,128)(2,1)} %bitcast.61, s32[128]{0:T(128)S(1)} %multiply_add_fusion), kind=kOutput, calls=%fused_computation.2 | convolution fusion | flops 618946560 | bytes 7864832 | tf_op jit(solution)/shard_map/st,ntc->snc/dot_general | solution.py:135
  8.1 9.7 %reshape.110 = bf16[64,3,4,4,768]{4,3,1,0,2:T(4,128)(2,1)} reshape(bf16[192,4,3072]{2,0,1:T(8,128)(2,1)} %convolution_convert_fusion) | data formatting | bytes 9437184 | tf_op jit(solution)/shard_map/reshape | solution.py:138
  17.9 10.6 %copy.67 = bf16[64,3,4,4,768]{4,2,1,3,0:T(4,128)(2,1)} copy(bf16[64,3,4,4,768]{4,3,1,0,2:T(4,128)(2,1)} %reshape.110) | data formatting | bytes 9437184 | tf_op jit(solution)/shard_map/reshape | solution.py:138
  28.4 16.9 %all-to-all-start = ((bf16[256,3,4,768]{3,2,1,0:T(4,128)(2,1)}), bf16[256,3,4,768]{3,2,1,0:T(4,128)(2,1)}, u32[]{:S(2)}, u32[]{:S(2)}) async-start(bf16[256,3,4,768]{3,2,1,0:T(4,128)(2,1)} %bitcast.51), calls=%async_computation | async-start | bytes 9437184 | tf_op jit(solution)/shard_map/all_to_all | solution.py:140
  45.4 10.3 %convert_reduce_fusion = s32[256,128]{1,0:T(8,128)S(1)} fusion(s32[256,128]{1,0:T(8,128)S(1)} %bitcast.57, pred[128,128]{1,0:T(8,128)(4,1)S(1)} %iota_compare_fusion.4), kind=kLoop, calls=%fused_computation | loop fusion | flops 16744448 | bytes 278528 | tf_op jit(solution)/shard_map/reduce_sum | solution.py:15
  56.3 97.6 %all-to-all-done = bf16[256,3,4,768]{3,2,1,0:T(4,128)(2,1)} async-done(((bf16[256,3,4,768]{3,2,1,0:T(4,128)(2,1)}), bf16[256,3,4,768]{3,2,1,0:T(4,128)(2,1)}, u32[]{:S(2)}, u32[]{:S(2)}) %all-to-all-start) | async-done | bytes 4718624 | tf_op jit(solution)/shard_map/all_to_all | solution.py:140
  153.8 35.7 %slice_reduce_fusion.1 = (bf16[256,3,768]{2,1,0:T(4,128)(2,1)}, bf16[256,3,768]{2,1,0:T(4,128)(2,1)}, bf16[256,3,768]{2,1,0:T(4,128)(2,1)S(1)}, bf16[256,3,768]{2,1,0:T(4,128)(2,1)S(1)}) fusion(bf16[4,256,3,768]{3,0,2,1:T(4,128)(2,1)} %bitcast.11), kind=kLoop, calls=%fused_computation.14 | loop fusion | bytes 9437184 | tf_op jit(solution)/shard_map/slice | solution.py:148
  189.5 2.2 squeeze.35
  192.9 2.9 fusion.108
  195.8 1.9 fusion.94
  200.1 3.9 squeeze.37
  204.0 2.5 fusion.155
  206.5 2.1 fusion.14
  209.0 6.8 %fusion.26 = (f32[768]{0:T(1024)}, f32[768]{0:T(1024)S(1)}, f32[768]{0:T(1024)}, f32[768]{0:T(1024)S(1)}, f32[768]{0:T(1024)S(1)}, /*index=5*/f32[768]{0:T(1024)S(1)}, f32[768,768]{0,1:T(8,128)}) fusion(f32[768,768]{0,1:T(8,128)S(1)} %get-tuple-element.46, f32[768]{0:T(1024)S(1)} %get-tuple-element.30, pred[768]{0:T(1024)(128)(4,1)} %copy-done.39, ...), kind=kOutput, calls=%fused_computation.54 | convolution fusion | flops 166325760 | bytes 14584832 | tf_op jit(solution)/shard_map/dot_general | solution.py:45
  215.9 2.9 fusion.56
  220.5 4.0 squeeze.36
  224.5 3.7 multiply_reduce_fusion.5
  228.3 2.3 multiply_convert_fusion.5
  231.8 2.0 fusion.28
  233.9 3.6 fusion.24
  237.5 1.9 fusion.55
  239.5 1.9 fusion.54
  241.4 1.9 fusion.53
  243.3 1.9 fusion.52
  245.2 1.9 fusion.51
  247.2 2.4 copy.83
  249.5 3.9 stack.38
  255.2 3.7 multiply_reduce_fusion.4
  258.9 3.3 multiply_convert_fusion.4
  264.0 3.7 multiply_reduce_fusion.3
  267.8 3.4 multiply_convert_fusion.3
  272.9 3.7 multiply_reduce_fusion.2
  276.6 3.3 multiply_convert_fusion.2
  281.7 2.9 multiply_reduce_fusion.1
  284.6 3.2 multiply_convert_fusion.1
  288.9 3.7 multiply_reduce_fusion
  292.6 2.7 multiply_convert_fusion
  300.0 2.5 fusion.30
  302.5 2.4 fusion.32
  309.7 2.0 stack.36
  317.6 2.5 copy.68
  320.1 3.7 stack.35
  323.8 7.2 %pad_maximum_fusion = bf16[256,3,4,768]{3,1,0,2:T(4,128)(2,1)S(1)} fusion(bf16[256,3,1,768]{3,1,0,2:T(4,128)(2,1)S(1)} %copy-done.6, bf16[256,3,1,768]{3,1,0,2:T(4,128)(2,1)S(1)} %stack.37, bf16[256,3,1,768]{3,1,0,2:T(4,128)(2,1)} %stack.36, bf16[256,3,1,768]{3,1,0,2:T(4,128)(2,1)} %stack.35), kind=kLoop, calls=%fused_computation.1 | loop fusion | flops 7077888 | bytes 9437184 | tf_op jit(solution)/shard_map/stack | solution.py:153
  331.1 6.1 %copy.84 = bf16[256,3,4,768]{3,2,1,0:T(4,128)(2,1)S(1)} copy(bf16[256,3,4,768]{3,1,0,2:T(4,128)(2,1)S(1)} %pad_maximum_fusion) | data formatting | bytes 9437184 | tf_op jit(solution)/shard_map/stack | solution.py:153
  337.2 116.2 %all_to_all.10 = bf16[256,3,4,768]{3,2,1,0:T(4,128)(2,1)S(1)} all-to-all(bf16[256,3,4,768]{3,2,1,0:T(4,128)(2,1)S(1)} %copy.84), channel_id=1, replica_groups=mesh['dp'=64,'seq'=4] {'dp','seq'}, dimensions={0} | all-to-all | bytes 9437184 | tf_op jit(solution)/shard_map/all_to_all | solution.py:155
  453.4 4.0 copy.107
  457.3 9.3 %reshape.113 = bf16[4,192,3072]{2,1,0:T(8,128)(2,1)} reshape(bf16[4,64,3,4,768]{4,3,2,1,0:T(4,128)(2,1)} %bitcast.53) | data formatting | bytes 9437184 | tf_op jit(solution)/shard_map/reshape | solution.py:157
  466.6 4.2 fusion
  (162 shorter events, 38.0 us)
Async XLA Ops:
  28.4 16.9 %copy-start.15 = (s32[32768,1]{0,1:T(1,128)S(1)}, s32[32768,1]{0,1:T(1,128)}, u32[]{:S(2)}) copy-start(s32[32768,1]{0,1:T(1,128)} %param.10) | copy-start | bytes 393220
  28.4 17.0 %copy-start.28 = (s32[32768]{0:T(1024)S(1)}, s32[32768]{0:T(1024)}, u32[]{:S(2)}) copy-start(s32[32768]{0:T(1024)} %param.11) | copy-start | bytes 393220
  28.4 125.4 %all-to-all-start = ((bf16[256,3,4,768]{3,2,1,0:T(4,128)(2,1)}), bf16[256,3,4,768]{3,2,1,0:T(4,128)(2,1)}, u32[]{:S(2)}, u32[]{:S(2)}) async-start(bf16[256,3,4,768]{3,2,1,0:T(4,128)(2,1)} %bitcast.51), calls=%async_computation | async-start | bytes 9437184 | tf_op jit(solution)/shard_map/all_to_all | solution.py:140
  56.2 150.3 %copy-start.39 = (pred[768]{0:T(1024)(128)(4,1)}, pred[768]{0:T(1024)(128)(4,1)S(1)}, u32[]{:S(2)}) copy-start(pred[768]{0:T(1024)(128)(4,1)S(1)} %broadcast_compare_fusion.1) | copy-start | bytes 2308
  192.9 2.9 copy-start.8
  208.7 7.2 %copy-start.48 = (f32[768,768]{0,1:T(8,128)}, f32[768,768]{0,1:T(8,128)S(1)}, u32[]{:S(2)}) copy-start(f32[768,768]{0,1:T(8,128)S(1)} %get-tuple-element.46) | copy-start | bytes 7077892
  208.7 7.2 %copy-start.51 = (f32[768]{0:T(1024)}, f32[768]{0:T(1024)S(1)}, u32[]{:S(2)}) copy-start(f32[768]{0:T(1024)S(1)} %get-tuple-element.30) | copy-start | bytes 9220
  208.7 7.2 %copy-start.54 = (f32[768]{0:T(1024)}, f32[768]{0:T(1024)S(1)}, u32[]{:S(2)}) copy-start(f32[768]{0:T(1024)S(1)} %get-tuple-element.31) | copy-start | bytes 9220
  209.0 6.8 %copy-start.40 = (pred[768]{0:T(1024)(128)(4,1)S(1)}, pred[768]{0:T(1024)(128)(4,1)}, u32[]{:S(2)}) copy-start(pred[768]{0:T(1024)(128)(4,1)} %copy-done.39) | copy-start | bytes 2308
  215.8 2.9 copy-start.58
  224.4 3.8 copy-start.7
  224.5 3.8 copy-start.11
  224.5 3.8 copy-start.41
  224.5 3.8 copy-start.55
  224.5 3.8 copy-start.59
  228.2 5.6 %copy-start.4 = (f32[768,768]{0,1:T(8,128)S(1)}, f32[768,768]{0,1:T(8,128)}, u32[]{:S(2)}) copy-start(f32[768,768]{0,1:T(8,128)} %fusion.94) | copy-start | bytes 7077892
  228.3 5.6 %copy-start.12 = (f32[768,768]{0,1:T(8,128)S(1)}, f32[768,768]{0,1:T(8,128)}, u32[]{:S(2)}) copy-start(f32[768,768]{0,1:T(8,128)} %get-tuple-element.47) | copy-start | bytes 7077892
  230.6 3.3 copy-start.1
  230.6 3.2 copy-start.31
  237.5 3.9 copy-start.33
  237.5 5.8 %copy-start.29 = (f32[768]{0:T(1024)}, f32[768]{0:T(1024)S(1)}, u32[]{:S(2)}) copy-start(f32[768]{0:T(1024)S(1)} %get-tuple-element.32) | copy-start | bytes 9220
  255.2 3.7 copy-start.13
  255.2 3.7 copy-start.32
  255.2 3.7 copy-start.38
  255.2 3.7 copy-start.42
  264.0 3.7 copy-start.5
  264.0 3.7 copy-start.36
  264.0 3.7 copy-start.43
  272.9 3.7 copy-start.2
  272.9 3.7 copy-start.34
  272.9 3.7 copy-start.44
  276.6 5.0 %copy-start.30 = (f32[768]{0:T(1024)S(1)}, f32[768]{0:T(1024)}, u32[]{:S(2)}) copy-start(f32[768]{0:T(1024)} %copy-done.29) | copy-start | bytes 9220
  281.7 2.9 copy-start.45
  288.9 3.7 copy-start.50
  288.9 3.7 copy-start.53
  288.9 3.7 copy-start.57
  292.6 3.3 copy-start.17
  295.3 2.8 copy-start.22
  300.0 4.9 %copy-start.9 = (bf16[768,768]{1,0:T(8,128)(2,1)S(1)}, bf16[768,768]{1,0:T(8,128)(2,1)}, u32[]{:S(2)}) copy-start(bf16[768,768]{1,0:T(8,128)(2,1)} %squeeze.35) | copy-start | bytes 3538948
  300.0 4.9 %copy-start.19 = (bf16[768,768]{0,1:T(8,128)(2,1)S(1)}, bf16[768,768]{0,1:T(8,128)(2,1)}, u32[]{:S(2)}) copy-start(bf16[768,768]{0,1:T(8,128)(2,1)} %multiply_convert_fusion.2) | copy-start | bytes 3538948
  300.0 6.0 %copy-start.21 = (bf16[768,768]{0,1:T(8,128)(2,1)S(1)}, bf16[768,768]{0,1:T(8,128)(2,1)}, u32[]{:S(2)}) copy-start(bf16[768,768]{0,1:T(8,128)(2,1)} %multiply_convert_fusion.1) | copy-start | bytes 3538948
  302.5 4.5 copy-start.23
  308.0 3.6 copy-start.24
  308.0 4.3 copy-start.25
  309.7 3.4 copy-start.26
  309.7 4.0 copy-start.27
  317.6 6.2 %copy-start.6 = (bf16[256,3,1,768]{3,1,0,2:T(4,128)(2,1)S(1)}, bf16[256,3,1,768]{3,1,0,2:T(4,128)(2,1)}, u32[]{:S(2)}) copy-start(bf16[256,3,1,768]{3,1,0,2:T(4,128)(2,1)} %stack.38) | copy-start | bytes 3538948
  457.3 9.3 %copy-start.47 = (s32[128]{0:T(128)S(1)}, s32[128]{0:T(128)}, u32[]{:S(2)}) copy-start(s32[128]{0:T(128)} %copy-done.46) | copy-start | bytes 1540
  (13 other events, 26.7 us)

commit v2 on v1

--- a/solution.py
+++ b/solution.py
@@ -1,6 +1,8 @@
 import jax
 import jax.numpy as jnp
 from jax import lax
+from jax.experimental import pallas as pl
+from jax.experimental.pallas import tpu as pltpu
 from jax.sharding import PartitionSpec as P
 
 HD = 128
@@ -107,7 +109,7 @@
     )
 
 
-def body(queries, keys, values, upstream, dest_group, clip_ids):
+def plain_path(queries, keys, values, upstream, dest_group, clip_ids):
     group_count = lax.axis_size("dp")
     part_count = lax.axis_size("seq")
     group_index = lax.axis_index("dp")
@@ -158,6 +160,373 @@
     all_home = return_rows(positions, slots, routed_back)
     return (all_home[0], all_home[1], all_home[2], all_home[3])
 
+PAGES = 14
+HEAVY_MAX = 12
+SPAN = 256
+MIB = 1 << 20
+NONE = -1.0
+F32 = jnp.float32
+BF16 = jnp.bfloat16
+PAIRS = (
+    (0, ((0, 0),)),
+    (1, ((1, 0),)),
+    (2, ((2, 0),)),
+    (3, ((3, 0),)),
+    (4, ((0, 1), (1, 2), (4, 3))),
+    (5, ((2, 1), (3, 2), (4, 4), (5, 5))),
+    (6, ((4, 6), (5, 7))),
+)
+CODES = 8
+
+
+def iota(shape, dim):
+    return lax.broadcasted_iota(jnp.int32, shape, dim)
+
+
+def dot(a, b, dims=(((1,), (0,)), ((), ()))):
+    return lax.dot_general(a, b, dims, preferred_element_type=F32)
+
+
+def page_codes(axis, heavy, heavy_rank):
+    shape = (128, 512) if axis == 0 else (512, 128)
+    place = iota(shape, 1 - axis)
+    index = iota(shape, axis)
+
+    def total(values):
+        return jnp.sum(values, axis=axis, keepdims=True).astype(jnp.int32)
+
+    light = (index < 64) & (heavy < 0.5)
+    home = place >> 3
+    line = iota((1, 512) if axis == 0 else (512, 1), 1 - axis)
+    own, second, array = line >> 3, (line >> 2) & 1, line & 3
+    is_heavy = total(jnp.where(index == home, heavy, 0.0)) > 0
+    below = total(jnp.where(index < home, heavy, 0.0))
+    heavies = total(jnp.where(index == index, heavy, 0.0))
+    rank = own - below
+    index_f = index.astype(F32)
+    heavy_rank_i = heavy_rank.astype(jnp.int32)
+    served = total(jnp.where((heavy > 0.5) & (heavy_rank_i == (rank >> 1)), index_f, 0.0))
+    eased = total(jnp.where(light & (index - heavy_rank_i == rank - 2 * heavies), index_f, 0.0))
+    is_light = jnp.logical_not(is_heavy)
+    role_a = is_light & (rank < 2 * heavies)
+    role_b = is_light & (rank >= 2 * heavies) & (rank < 4 * heavies)
+    odd = (rank & 1) == 1
+    even = jnp.logical_not(odd)
+    not_a = is_light & (rank >= 2 * heavies)
+    first = second == 0
+
+    def code(cond, group, slot):
+        return jnp.where(cond, 4 * (3 * group + slot) + array, -1)
+
+    codes = (
+        4 * (3 * own + second) + array,
+        code(is_heavy & first, own, 2),
+        code(is_heavy & jnp.logical_not(first), own, 2),
+        code(is_light, own, second),
+        code(role_a & even, served, second),
+        jnp.maximum(code(role_a & odd, served, second), code(not_a, own, second)),
+        code(role_a & even & first, served, 2),
+        jnp.maximum(code(role_a & odd & first, served, 2), code(role_b, eased, second)),
+    )
+    return tuple(c.astype(F32) for c in codes)
+
+
+def pack_kernel(me_ref, targets_ref, q_ref, k_ref, v_ref, u_ref, send_ref, codes_ref, home_ref, info_ref):
+    device, group = me_ref[0], me_ref[1]
+    targets = targets_ref[...]
+    lane = iota((SPAN, 128), 1)
+    ones = jnp.ones((128, 128), BF16)
+    flags = jnp.zeros((SPAN, 128), jnp.int32)
+    shift = 2 * (lane & 7)
+    spread = jnp.left_shift(jnp.ones((SPAN, 128), jnp.int32), 2 * (targets & 7))
+    for word in range(8):
+        bits = jnp.where((targets >> 3) == word, spread, 0).astype(F32).astype(BF16)
+        counts = dot(bits, ones).astype(jnp.int32)
+        three = jnp.right_shift(counts, shift) & jnp.right_shift(counts, shift + 1) & 1
+        flags = jnp.where((lane >> 3) == word, three, flags)
+    heavy = jnp.max(flags.astype(F32), axis=0, keepdims=True)
+    square = (128, 128)
+    row, col = iota(square, 0), iota(square, 1)
+    heavy_l = jnp.broadcast_to(heavy, square)
+    earlier = jnp.where(row < col, 1.0, 0.0).astype(BF16)
+    rank_l = dot(heavy_l.astype(BF16), earlier)
+    heavy_c, rank_c = heavy_l.T, rank_l.T
+    codes_c = page_codes(1, heavy_l[:1], rank_l[:1])
+    codes_l = page_codes(0, heavy_c[:, :1], rank_c[:, :1])
+    for n in range(CODES):
+        codes_ref[n : n + 1, :] = codes_l[n]
+
+    mine = jnp.broadcast_to(targets_ref[pl.ds(device, 1), :].astype(F32), square)
+    mine_c = mine.T
+    same = mine == mine_c
+    prior_l = jnp.sum(jnp.where(same & (row < col), 1.0, 0.0), axis=0, keepdims=True)
+    prior_c = jnp.sum(jnp.where(same & (col < row), 1.0, 0.0), axis=1, keepdims=True)
+    key_l = 12.0 * mine[:1] + 4.0 * prior_l
+    key_c = 12.0 * mine_c + 4.0 * prior_c
+    key_l = jnp.concatenate([key_l + float(a) for a in range(4)], axis=1)
+    for a in range(4):
+        home_ref[a * 128 : (a + 1) * 128, :] = key_c + float(a)
+
+    def pick(n):
+        return jnp.where(codes_c[n] == key_l, 1.0, 0.0).astype(BF16)
+
+    def columns(head):
+        return jnp.concatenate(
+            [
+                jnp.concatenate(
+                    [ref[:, (6 * x + head) * HD : (6 * x + head + 1) * HD] for x in range(4)], axis=1
+                )
+                for ref in (q_ref, k_ref, v_ref, u_ref)
+            ],
+            axis=0,
+        )
+
+    pickers = [pick(n) for n in range(CODES)]
+    for pair, parts in PAIRS:
+        total = None
+        for head, n in parts:
+            term = dot(pickers[n], columns(head))
+            total = term if total is None else total + term
+        for x in range(4):
+            tile = total[:, x * 128 : (x + 1) * 128].reshape(64, 8, 128)
+            send_ref[:, x, 8 * pair : 8 * pair + 8, :] = tile.astype(BF16)
+
+    lane1 = iota((1, 128), 1)
+    heavy1, rank1 = heavy_l[:1], rank_l[:1]
+
+    def scalar(values):
+        return jnp.sum(values).astype(jnp.int32)
+
+    heavies = scalar(heavy1)
+    is_heavy = scalar(jnp.where(lane1 == group, heavy1, 0.0))
+    rank = group - scalar(jnp.where(lane1 < group, heavy1, 0.0))
+    lane_f = lane1.astype(F32)
+    rank1_i = rank1.astype(jnp.int32)
+    served = scalar(jnp.where((heavy1 > 0.5) & (rank1_i == (rank >> 1)), lane_f, 0.0))
+    light1 = (heavy1 < 0.5) & (lane1 < 64)
+    eased = scalar(jnp.where(light1 & (lane1 - rank1_i == rank - 2 * heavies), lane_f, 0.0))
+    role_a = (is_heavy == 0) & (rank < 2 * heavies)
+    role_b = (is_heavy == 0) & (rank >= 2 * heavies) & (rank < 4 * heavies)
+    info_ref[0] = heavies
+    info_ref[1] = jnp.where(is_heavy > 0, 0, jnp.where(role_a, 5, jnp.where(role_b, 7, 6)))
+    info_ref[2] = jnp.where(is_heavy > 0, 4, jnp.where(role_a, 1, 0))
+    info_ref[3] = jnp.where(role_a, served, jnp.where(role_b, eased, group))
+    info_ref[4] = group
+    info_ref[5] = is_heavy
+
+
+def label_kernel(info_ref, targets_ref, clips_ref, col_ref, row_ref):
+    targets = targets_ref[...]
+    clips = clips_ref[...] + 1
+    row, col = iota((128, 128), 0), iota((128, 128), 1)
+    earlier = jnp.where(row < col, 1.0, 0.0).astype(BF16)
+    ones = jnp.ones((128, 128), BF16)
+    for n in range(2):
+        arriving = targets == info_ref[4 - n]
+        rank = dot(jnp.where(arriving, 1.0, 0.0).astype(BF16), earlier).astype(jnp.int32)
+        for slot in range(3):
+            labels = jnp.where(arriving & (rank == slot), clips, 0).astype(F32).astype(BF16)
+            col_ref[n, slot * SPAN : (slot + 1) * SPAN, :] = dot(labels, ones)
+            row_ref[n, :, slot * SPAN : (slot + 1) * SPAN] = dot(
+                ones[:8], labels, (((1,), (1,)), ((), ()))
+            )
+
+
+def attend_unit(d_ref, e_ref, col_ref, row_ref, start, third, which, count):
+    scale = HD**-0.5
+    rows_t = (((1,), (1,)), ((), ()))
+    cols_t = (((0,), (0,)), ((), ()))
+    places = [start, start + SPAN] + ([third] if count == 3 else [])
+
+    def load(a):
+        return jnp.concatenate([d_ref[a, pl.ds(place, SPAN), :] for place in places], axis=0)
+
+    key, value = load(1), load(2)
+    row_labels = row_ref[which, 0:1, : count * SPAN]
+    grad_key, grad_value = None, None
+    for n, place in enumerate(places):
+        query = d_ref[0, pl.ds(place, SPAN), :]
+        cotangent = d_ref[3, pl.ds(place, SPAN), :]
+        labels = col_ref[which, n * SPAN : (n + 1) * SPAN, :]
+        related = jnp.concatenate([labels] * (2 * count), axis=1) == row_labels
+        scores = jnp.where(related, dot(query, key, rows_t), -1e30)
+        top = jnp.max(scores, axis=1, keepdims=True)
+        weights = jnp.exp2((scores - top) * (scale * 1.4426950408889634))
+        probs = weights * (1.0 / jnp.sum(weights, axis=1, keepdims=True))
+        probs_b = probs.astype(BF16)
+        attended = dot(probs_b, value).astype(BF16)
+        delta = jnp.sum(cotangent.astype(F32) * attended.astype(F32), axis=1, keepdims=True)
+        dscores = (probs * (dot(cotangent, value, rows_t) - delta)).astype(BF16)
+        e_ref[0, pl.ds(place, SPAN), :] = attended
+        e_ref[1, pl.ds(place, SPAN), :] = (dot(dscores, key) * scale).astype(BF16)
+        term_key = dot(dscores, query, cols_t)
+        term_value = dot(probs_b, cotangent, cols_t)
+        grad_key = term_key if n == 0 else grad_key + term_key
+        grad_value = term_value if n == 0 else grad_value + term_value
+    for n, place in enumerate(places):
+        part = slice(n * SPAN, (n + 1) * SPAN)
+        e_ref[2, pl.ds(place, SPAN), :] = (grad_key[part] * scale).astype(BF16)
+        e_ref[3, pl.ds(place, SPAN), :] = grad_value[part].astype(BF16)
+
+
+def attend_kernel(info_ref, col_ref, row_ref, came_ref, out_ref, d_ref, e_ref):
+    row, col = iota((SPAN, SPAN), 0), iota((SPAN, SPAN), 1)
+    apart = jnp.where(((row & 31) << 3) + (row >> 5) == col, 1.0, 0.0).astype(BF16)
+    together = jnp.where(((col & 31) << 3) + (col >> 5) == row, 1.0, 0.0).astype(BF16)
+
+    def split(block, carry):
+        base = pl.multiple_of(block * 32, 32)
+        rows = jnp.concatenate(
+            [
+                came_ref[pl.ds(base, 32), 8 * j : 8 * j + 8, :].astype(F32).reshape(SPAN, 128)
+                for j in range(7)
+            ],
+            axis=1,
+        ).astype(BF16)
+        parted = dot(apart, rows).astype(BF16)
+        for j in range(7):
+            for i in range(2):
+                for a in range(4):
+                    at = (4 * i + a) * 32
+                    d_ref[a, pl.ds(pl.multiple_of((2 * j + i) * SPAN + base, 32), 32), :] = parted[
+                        at : at + 32, j * 128 : (j + 1) * 128
+                    ]
+        return carry
+
+    lax.fori_loop(0, 8, split, 0)
+    for b in range(4):
+        e_ref[b, 12 * SPAN :, :] = jnp.zeros((2 * SPAN, 128), BF16)
+
+    def pages_of_two(it, carry):
+        start = pl.multiple_of(it * (2 * SPAN), 2 * SPAN)
+        attend_unit(d_ref, e_ref, col_ref, row_ref, start, None, it // 6, 2)
+        return carry
+
+    def pages_of_three(it, carry):
+        is_heavy = info_ref[5]
+        start = pl.multiple_of(jnp.where(is_heavy > 0, it * (2 * SPAN), 10 * SPAN), 2 * SPAN)
+        third = pl.multiple_of(jnp.where(is_heavy > 0, (8 + it) * SPAN, 12 * SPAN), SPAN)
+        attend_unit(d_ref, e_ref, col_ref, row_ref, start, third, 1 - is_heavy, 3)
+        return carry
+
+    lax.fori_loop(0, info_ref[1], pages_of_two, 0)
+    lax.fori_loop(0, info_ref[2], pages_of_three, 0)
+
+    def join(block, carry):
+        base = pl.multiple_of(block * 32, 32)
+        rows = jnp.concatenate(
+            [
+                jnp.concatenate(
+                    [
+                        e_ref[b, pl.ds(pl.multiple_of((2 * j + i) * SPAN + base, 32), 32), :]
+                        for i in range(2)
+                        for b in range(4)
+                    ],
+                    axis=0,
+                )
+                for j in range(7)
+            ],
+            axis=1,
+        )
+        joined = dot(together, rows)
+        for j in range(7):
+            tile = joined[:, j * 128 : (j + 1) * 128].reshape(32, 8, 128)
+            out_ref[pl.ds(base, 32), 8 * j : 8 * j + 8, :] = tile.astype(BF16)
+        return carry
+
+    lax.fori_loop(0, 8, join, 0)
+
+
+def home_kernel(codes_ref, home_ref, back_ref, o_ref, dq_ref, dk_ref, dv_ref):
+    home = home_ref[...]
+    home = jnp.concatenate([home] * 4, axis=1)
+    pickers = [
+        jnp.where(home == codes_ref[n : n + 1, :], 1.0, 0.0).astype(BF16) for n in range(CODES)
+    ]
+    for head in range(6):
+        total = None
+        for pair, parts in PAIRS:
+            for part_head, n in parts:
+                if part_head == head:
+                    rows = jnp.concatenate(
+                        [
+                            back_ref[:, x, 8 * pair : 8 * pair + 8, :].astype(F32).reshape(512, 128)
+                            for x in range(4)
+                        ],
+                        axis=1,
+                    ).astype(BF16)
+                    term = dot(pickers[n], rows)
+                    total = term if total is None else total + term
+        for b, ref in enumerate((o_ref, dq_ref, dk_ref, dv_ref)):
+            for x in range(4):
+                at = (6 * x + head) * HD
+                ref[:, at : at + HD] = total[
+                    b * 128 : (b + 1) * 128, x * 128 : (x + 1) * 128
+                ].astype(BF16)
+
+
+def body(queries, keys, values, upstream, dest_group, clip_ids):
+    group = lax.axis_index("dp")
+    device = group * 4 + lax.axis_index("seq")
+    targets = dest_group.reshape(SPAN, 128)
+    clips = clip_ids.reshape(SPAN, 128)
+    me = jnp.stack((device, group)).astype(jnp.int32)
+    vmem = pl.BlockSpec(memory_space=pltpu.VMEM)
+    smem = pl.BlockSpec(memory_space=pltpu.SMEM)
+    params = pltpu.CompilerParams(vmem_limit_bytes=40 * MIB)
+    shape = jax.ShapeDtypeStruct
+    send, codes, home, info = pl.pallas_call(
+        pack_kernel,
+        out_shape=(
+            shape((64, 4, 4 * PAGES, 128), BF16),
+            shape((CODES, 512), F32),
+            shape((512, 128), F32),
+            shape((8,), jnp.int32),
+        ),
+        in_specs=[smem] + [vmem] * 5,
+        out_specs=(vmem, vmem, vmem, smem),
+        compiler_params=params,
+    )(me, targets, queries, keys, values, upstream)
+
+    def paged_path():
+        came = lax.all_to_all(
+            send.reshape(SPAN, 4 * PAGES, 128), ("dp", "seq"), split_axis=0, concat_axis=0, tiled=True
+        )
+        col, row = pl.pallas_call(
+            label_kernel,
+            out_shape=(shape((2, 3 * SPAN, 128), F32), shape((2, 8, 3 * SPAN), F32)),
+            in_specs=[smem, vmem, vmem],
+            out_specs=(vmem, vmem),
+            compiler_params=params,
+        )(info, targets, clips)
+        out = pl.pallas_call(
+            attend_kernel,
+            out_shape=shape((SPAN, 4 * PAGES, 128), BF16),
+            in_specs=[smem, vmem, vmem, vmem],
+            out_specs=vmem,
+            scratch_shapes=[
+                pltpu.VMEM((4, PAGES * SPAN, 128), BF16),
+                pltpu.VMEM((4, PAGES * SPAN, 128), BF16),
+            ],
+            compiler_params=params,
+        )(info, col, row, came)
+        back = lax.all_to_all(out, ("dp", "seq"), split_axis=0, concat_axis=0, tiled=True)
+        return tuple(
+            pl.pallas_call(
+                home_kernel,
+                out_shape=(shape(queries.shape, BF16),) * 4,
+                in_specs=[vmem] * 3,
+                out_specs=(vmem,) * 4,
+                compiler_params=params,
+            )(codes, home, back.reshape(64, 4, 4 * PAGES, 128))
+        )
+
+    return lax.cond(
+        info[0] <= HEAVY_MAX,
+        paged_path,
+        lambda: plain_path(queries, keys, values, upstream, dest_group, clip_ids),
+    )
+
 
 def solution(mesh):
     return jax.shard_map(

time: 485 us -> 232 us (0.48); the launches traced: 476 us -> 232 us
  local copies, waits for them, and re-layouts: 130 us -> 0.7 us
  matrix products: 91.9 us -> 0 us
  Pallas kernels: 0 us -> 35.2 us
  blocking collectives: 116 us -> 93.1 us
  other arithmetic: 22.2 us -> 0.08 us
  waiting for transfers between devices: 97.6 us -> 84.9 us
    dot_general x38 -> x0, matrix products: 91.9 us -> none  [the longest x6 21.5 us: attend_forward(): jnp.dot(probs_b, value_head, preferred_element_type=jnp.float32)]
    slice x1 -> x0, local copies, waits for them, and re-layouts: 35.7 us -> none  [body(): regrouped[2]]
    pallas_call x0 -> x4, Pallas kernels: none -> 35.2 us  [the longest x1 19.6 us: paged_path(): pl.pallas_call(attend_kernel, out_shape=shape((SPAN, 4 * PAGES, 128), BF1...]
    reshape x4 -> x0, local copies, waits for them, and re-layouts: 33.6 us -> none  [the longest x2 20.3 us: body(): blocks = packed.reshape(group_count, capacity, 4, part_count, width)]
    all_to_all x1, blocking collectives: 116 us -> 93.1 us  [paged_path(): lax.all_to_all(out, ('dp', 'seq'), split_axis=0, concat_axis=0, tiled=True)]
    unnamed x136 -> x10, local copies, waits for them, and re-layouts: 23 us -> 0.03 us
    another operation x5 -> x0, local copies, waits for them, and re-layouts: 16.2 us -> none  [body(): jnp.stack((attended, gradients[0], gradients[1], gradients[2]), axis=1)]
    reduce_sum x4 -> x0, other arithmetic: 14.3 us -> none  [the longest x2 10.4 us: prior_count(): return jnp.sum((matching & earlier).astype(jnp.int32), axis=-1)]
  transfers between devices with their start and end apart: 1 -> 1, of which waited for: 1 -> 1; matrix products, arithmetic and copies ran while one was open for 2% -> 0% of each run, Pallas kernels for 0% -> 1%
where the time goes in v2:
time: 232 us
  blocking collectives  93.1 us (40%)
  waiting for transfers between devices  84.9 us (37%)
  Pallas kernels  35.2 us (15%)
  starting transfers between devices  16.5 us (7%)
    all_to_all x1, blocking collectives, paged_path(): lax.all_to_all(out, ('dp', 'seq'), split_axis=0, concat_axis=0, tiled=True)  93.1 us
    all_to_all x1, waiting for transfers between devices, paged_path(): lax.all_to_all(send.reshape(SPAN, 4 * PAGES, 128), ('dp', 'seq'), split_a...  84.9 us
    pallas_call x1, Pallas kernels, paged_path(): pl.pallas_call(attend_kernel, out_shape=shape((SPAN, 4 * PAGES, 128), BF1...  19.6 us
    all_to_all x1, starting transfers between devices, paged_path(): lax.all_to_all(send.reshape(SPAN, 4 * PAGES, 128), ('dp', 'seq'), split_a...  16.5 us
    pallas_call x1, Pallas kernels, body(): pl.pallas_call(pack_kernel, out_shape=(shape((64, 4, 4 * PAGES, 128), BF1...  8.88 us
    pallas_call x1, Pallas kernels, paged_path(): pl.pallas_call(home_kernel, out_shape=(shape(queries.shape, BF16),) * 4,...  5.24 us
  transfers between devices with their start and end apart: 1, of which 1 were waited for; matrix products, arithmetic and copies ran while one was open for 0% of the time, Pallas kernels for 1%

profile of v2, /device:TPU:1, one launch (start us, length us, event | category | flops | bytes accessed | tf_op | source)
XLA Modules:
  0.0 231.5 jit_solution(12443009167209768125)
XLA Ops:
  0.6 0.0 copy-start.8
  0.6 0.0 copy-start.25
  0.7 0.0 copy-start.26
  0.7 0.0 copy-start.27
  0.7 0.0 copy-start.28
  0.7 0.1 pad_add_fusion.me_ref
  0.8 8.9 %shard_map.101 = (bf16[64,4,56,128]{3,2,1,0:T(8,128)(2,1)}, f32[8,512]{1,0:T(8,128)}, f32[512,128]{1,0:T(8,128)}, s32[8]{0:T(128)S(1)}) custom-call(s32[2]{0:T(128)S(1)} %pad_add_fusion.me_ref, s32[256,128]{1,0:T(8,128)} %bitcast.64, bf16[128,3072]{1,0:T(8,128)(2,1)} %q_ref.1, bf16[128,3072]{1,0:T(8,128)(2,1)} %k_ref.1, bf16[128,3072]{1,0:T(8,128)(2,1)} %v_ref.1, ...), custom_call_target="tpu_custom_call" | custom-call | tf_op jit(solution)/shard_map/pallas_call | solution.py:478
  9.7 0.0 copy-done.8
  9.7 0.0 copy-done.25
  9.7 0.0 copy-done.26
  9.7 0.0 copy-done.27
  9.7 0.0 copy-done.28
  9.7 221.8 %conditional.1 = ((bf16[128,3072]{1,0:T(8,128)(2,1)}, bf16[128,3072]{1,0:T(8,128)(2,1)}, bf16[128,3072]{1,0:T(8,128)(2,1)}, bf16[128,3072]{1,0:T(8,128)(2,1)})) conditional(s32[]{:T(128)} %bitcast.26, (s32[32768,1]{0,1:T(1,128)S(1)}, s32[32768]{0:T(1024)}, bf16[128,3072]{1,0:T(8,128)(2,1)S(1)}, bf16[128,3072]{1,0:T(8,128)(2,1)S(1)}, ...), branch_computations={%region_0.22_spmd, %region_22.23_spmd} | conditional | flops 6839240704 | bytes 459571264 | solution.py:524
  10.0 0.0 copy-start.54
  10.0 0.0 copy-start.9
  10.0 0.5 copy-done.54
  10.5 0.0 copy-start.30
  10.5 0.0 copy-start.55
  10.5 0.2 copy-done.9
  10.7 16.5 %all-to-all-start = ((bf16[256,56,128]{2,1,0:T(8,128)(2,1)}), bf16[256,56,128]{2,1,0:T(8,128)(2,1)}, u32[]{:S(2)}, u32[]{:S(2)}) async-start(bf16[256,56,128]{2,1,0:T(8,128)(2,1)} %bitcast.63), calls=%async_computation | async-start | bytes 7340032 | tf_op jit(solution)/shard_map/cond/branch_1_fun/all_to_all | solution.py:492
  27.2 0.0 copy-done.30
  27.2 0.0 copy-done.55
  27.2 1.5 branch_1_fun.3
  28.7 84.9 %all-to-all-done.came_ref = bf16[256,56,128]{2,1,0:T(8,128)(2,1)} async-done(((bf16[256,56,128]{2,1,0:T(8,128)(2,1)}), bf16[256,56,128]{2,1,0:T(8,128)(2,1)}, u32[]{:S(2)}, u32[]{:S(2)}) %all-to-all-start) | async-done | bytes 3670048 | tf_op jit(solution)/shard_map/cond/branch_1_fun/all_to_all | solution.py:492
  113.6 19.6 %branch_1_fun.4 = bf16[256,56,128]{2,1,0:T(8,128)(2,1)S(1)} custom-call(s32[8]{0:T(128)S(1)} %copy-done.55, f32[2,768,128]{2,1,0:T(8,128)S(1)} %get-tuple-element.36.col_ref, f32[2,8,768]{2,1,0:T(8,128)S(1)} %get-tuple-element.37.row_ref, bf16[256,56,128]{2,1,0:T(8,128)(2,1)} %all-to-all-done.came_ref), custom_call_target="tpu_custom_call" | custom-call | tf_op jit(solution)/shard_map/cond/branch_1_fun/pallas_call | solution.py:502
  133.2 0.0 copy-start.31
  133.2 0.0 copy-start.36
  133.2 93.1 %all_to_all.17 = bf16[256,56,128]{2,1,0:T(8,128)(2,1)S(1)} all-to-all(bf16[256,56,128]{2,1,0:T(8,128)(2,1)S(1)} %branch_1_fun.4), channel_id=1, replica_groups=mesh['dp'=64,'seq'=4] {'dp','seq'}, dimensions={0} | all-to-all | bytes 7340032 | tf_op jit(solution)/shard_map/cond/branch_1_fun/all_to_all | solution.py:513
  226.3 0.0 copy-done.31
  226.3 0.0 copy-done.36
  226.3 5.2 %branch_1_fun.5 = (bf16[128,3072]{1,0:T(8,128)(2,1)}, bf16[128,3072]{1,0:T(8,128)(2,1)}, bf16[128,3072]{1,0:T(8,128)(2,1)}, bf16[128,3072]{1,0:T(8,128)(2,1)}) custom-call(f32[8,512]{1,0:T(8,128)S(1)} %copy-done.36, f32[512,128]{1,0:T(8,128)S(1)} %copy-done.31, bf16[64,4,56,128]{3,2,1,0:T(8,128)(2,1)S(1)} %bitcast.59), custom_call_target="tpu_custom_call" | custom-call | tf_op jit(solution)/shard_map/cond/branch_1_fun/pallas_call | solution.py:515
Async XLA Ops:
  0.6 9.1 %copy-start.8 = (s32[32768,1]{0,1:T(1,128)S(1)}, s32[32768,1]{0,1:T(1,128)}, u32[]{:S(2)}) copy-start(s32[32768,1]{0,1:T(1,128)} %param.12) | copy-start | bytes 393220
  0.6 9.1 %copy-start.25 = (bf16[128,3072]{1,0:T(8,128)(2,1)S(1)}, bf16[128,3072]{1,0:T(8,128)(2,1)}, u32[]{:S(2)}) copy-start(bf16[128,3072]{1,0:T(8,128)(2,1)} %q_ref.1) | copy-start | bytes 2359300
  0.7 9.1 %copy-start.26 = (bf16[128,3072]{1,0:T(8,128)(2,1)S(1)}, bf16[128,3072]{1,0:T(8,128)(2,1)}, u32[]{:S(2)}) copy-start(bf16[128,3072]{1,0:T(8,128)(2,1)} %k_ref.1) | copy-start | bytes 2359300
  0.7 9.1 %copy-start.27 = (bf16[128,3072]{1,0:T(8,128)(2,1)S(1)}, bf16[128,3072]{1,0:T(8,128)(2,1)}, u32[]{:S(2)}) copy-start(bf16[128,3072]{1,0:T(8,128)(2,1)} %v_ref.1) | copy-start | bytes 2359300
  0.7 9.1 %copy-start.28 = (bf16[128,3072]{1,0:T(8,128)(2,1)S(1)}, bf16[128,3072]{1,0:T(8,128)(2,1)}, u32[]{:S(2)}) copy-start(bf16[128,3072]{1,0:T(8,128)(2,1)} %u_ref.1) | copy-start | bytes 2359300
  10.0 0.5 copy-start.54
  10.0 0.7 copy-start.9
  10.5 16.7 %copy-start.30 = (s32[32768]{0:T(1024)S(1)}, s32[32768]{0:T(1024)}, u32[]{:S(2)}) copy-start(s32[32768]{0:T(1024)} %get-tuple-element.35) | copy-start | bytes 393220 | tf_op jit(solution)/shard_map/cond
  10.5 16.7 %copy-start.55 = (s32[8]{0:T(128)S(1)}, s32[8]{0:T(128)}, u32[]{:S(2)}) copy-start(s32[8]{0:T(128)} %copy-done.54) | copy-start | bytes 100 | tf_op jit(solution)/shard_map/cond
  10.7 102.9 %all-to-all-start = ((bf16[256,56,128]{2,1,0:T(8,128)(2,1)}), bf16[256,56,128]{2,1,0:T(8,128)(2,1)}, u32[]{:S(2)}, u32[]{:S(2)}) async-start(bf16[256,56,128]{2,1,0:T(8,128)(2,1)} %bitcast.63), calls=%async_computation | async-start | bytes 7340032 | tf_op jit(solution)/shard_map/cond/branch_1_fun/all_to_all | solution.py:492
  133.2 93.1 %copy-start.31 = (f32[512,128]{1,0:T(8,128)S(1)}, f32[512,128]{1,0:T(8,128)}, u32[]{:S(2)}) copy-start(f32[512,128]{1,0:T(8,128)} %get-tuple-element.32.home_ref) | copy-start | bytes 786436 | tf_op jit(solution)/shard_map/cond
  133.2 93.1 %copy-start.36 = (f32[8,512]{1,0:T(8,128)S(1)}, f32[8,512]{1,0:T(8,128)}, u32[]{:S(2)}) copy-start(f32[8,512]{1,0:T(8,128)} %get-tuple-element.31.codes_ref) | copy-start | bytes 49156 | tf_op jit(solution)/shard_map/cond

commit v3 on v1

--- a/solution.py
+++ b/solution.py
@@ -1,6 +1,8 @@
 import jax
 import jax.numpy as jnp
 from jax import lax
+from jax.experimental import pallas as pl
+from jax.experimental.pallas import tpu as pltpu
 from jax.sharding import PartitionSpec as P
 
 HD = 128
@@ -107,7 +109,7 @@
     )
 
 
-def body(queries, keys, values, upstream, dest_group, clip_ids):
+def plain_path(queries, keys, values, upstream, dest_group, clip_ids):
     group_count = lax.axis_size("dp")
     part_count = lax.axis_size("seq")
     group_index = lax.axis_index("dp")
@@ -158,6 +160,396 @@
     all_home = return_rows(positions, slots, routed_back)
     return (all_home[0], all_home[1], all_home[2], all_home[3])
 
+UNITS = 6
+PAGES = 13
+TRADES = UNITS - 1
+SPAN = 256
+MIB = 1 << 20
+F32 = jnp.float32
+BF16 = jnp.bfloat16
+ROWS_T = (((1,), (1,)), ((), ()))
+COLS_T = (((0,), (0,)), ((), ()))
+
+
+def iota(shape, dim):
+    return lax.broadcasted_iota(jnp.int32, shape, dim)
+
+
+def dot(a, b, dims=(((1,), (0,)), ((), ()))):
+    return lax.dot_general(a, b, dims, preferred_element_type=F32)
+
+
+def unit_table(heavy, heavy_rank):
+    square = (128, 128)
+    group, lane = iota(square, 0), iota(square, 1)
+
+    def total(cond, values):
+        return jnp.sum(jnp.where(cond, values, 0.0), axis=1, keepdims=True).astype(jnp.int32)
+
+    heavy_rank = heavy_rank.astype(jnp.int32)
+    lane_f = lane.astype(F32)
+    is_heavy = total(lane == group, heavy) > 0
+    below = total(lane < group, heavy)
+    heavies = total(lane >= 0, heavy)
+    rank = group[:, :1] - below
+    light = (lane < 64) & (heavy < 0.5)
+    trades = jnp.logical_not(is_heavy) & (rank < TRADES * heavies)
+    turn = (rank * 13) >> 6
+    served = total((heavy > 0.5) & (heavy_rank == turn), lane_f)
+    third = jnp.where(is_heavy, 0, jnp.where(trades, rank - TRADES * turn + 1, -1))
+    table = jnp.zeros(square, jnp.int32)
+    for unit in range(UNITS):
+        source = group[:, :1]
+        if unit > 0:
+            light_rank = lane - heavy_rank
+            traded = total(light & (light_rank == TRADES * below + unit - 1), lane_f)
+            source = jnp.where(is_heavy, traded, jnp.where(third == unit, served, source))
+        table = jnp.where(lane == unit, source, table)
+        table = jnp.where(lane == UNITS + unit, jnp.where(third == unit, 3 * source + 2, -1), table)
+    return jnp.where(lane == 2 * UNITS, third, table), heavies
+
+
+def pack_kernel(
+    me_ref, targets_ref, q_ref, k_ref, v_ref, u_ref, send_ref, codes_ref, thirds_ref, home_ref, info_ref
+):
+    device, group = me_ref[0], me_ref[1]
+    targets = targets_ref[...]
+    lane = iota((SPAN, 128), 1)
+    ones = jnp.ones((128, 128), BF16)
+    flags = jnp.zeros((SPAN, 128), jnp.int32)
+    shift = 2 * (lane & 7)
+    spread = jnp.left_shift(jnp.ones((SPAN, 128), jnp.int32), 2 * (targets & 7))
+    for word in range(8):
+        bits = jnp.where((targets >> 3) == word, spread, 0).astype(F32).astype(BF16)
+        counts = dot(bits, ones).astype(jnp.int32)
+        three = jnp.right_shift(counts, shift) & jnp.right_shift(counts, shift + 1) & 1
+        flags = jnp.where((lane >> 3) == word, three, flags)
+    heavy = jnp.max(flags.astype(F32), axis=0, keepdims=True)
+    square = (128, 128)
+    row, col = iota(square, 0), iota(square, 1)
+    heavy = jnp.broadcast_to(heavy, square)
+    earlier = jnp.where(row < col, 1.0, 0.0).astype(BF16)
+    table, heavies = unit_table(heavy, dot(heavy.astype(BF16), earlier))
+
+    table_f = table.astype(F32)
+    table_b = table_f.astype(BF16)
+    table_t = table_f.T[:16].astype(BF16)
+    spread_c = jnp.where(iota((512, 128), 0) >> 3 == iota((512, 128), 1), 1.0, 0.0).astype(BF16)
+    spread_l = jnp.where(iota((128, 512), 1) >> 3 == iota((128, 512), 0), 1.0, 0.0).astype(BF16)
+    thirds_c = jnp.where(iota((256, 128), 0) >> 2 == iota((256, 128), 1), 1.0, 0.0).astype(BF16)
+    thirds_l = jnp.where(iota((128, 256), 1) >> 2 == iota((128, 256), 0), 1.0, 0.0).astype(BF16)
+
+    def two(line):
+        return (4 * ((line >> 2) & 1) + (line & 3)).astype(F32)
+
+    def one(codes, line):
+        return jnp.where(codes < 0.0, -1.0, 4.0 * codes + (line & 3).astype(F32))
+
+    pages_c = 12.0 * dot(spread_c, table_b) + two(iota((512, 128), 0))
+    pages_l = 12.0 * dot(table_t, spread_l) + two(iota((16, 512), 1))
+    third_c = one(dot(thirds_c, table_b), iota((256, 128), 0))
+    third_l = one(dot(table_t, thirds_l), iota((16, 256), 1))
+    codes_ref[...] = pages_l[:8]
+    thirds_ref[...] = third_l[UNITS : UNITS + 8]
+
+    mine = jnp.broadcast_to(targets_ref[pl.ds(device, 1), :].astype(F32), square)
+    mine_c = mine.T
+    same = mine == mine_c
+    prior_l = jnp.sum(jnp.where(same & (row < col), 1.0, 0.0), axis=0, keepdims=True)
+    prior_c = jnp.sum(jnp.where(same & (col < row), 1.0, 0.0), axis=1, keepdims=True)
+    key_l = 12.0 * mine[:1] + 4.0 * prior_l
+    key_c = 12.0 * mine_c + 4.0 * prior_c
+    key_l = jnp.concatenate([key_l + float(a) for a in range(4)], axis=1)
+    for a in range(4):
+        home_ref[a * 128 : (a + 1) * 128, :] = key_c + float(a)
+
+    extra = None
+    for unit in range(UNITS):
+        columns = jnp.concatenate(
+            [
+                jnp.concatenate(
+                    [ref[:, (6 * x + unit) * HD : (6 * x + unit + 1) * HD] for x in range(4)], axis=1
+                )
+                for ref in (q_ref, k_ref, v_ref, u_ref)
+            ],
+            axis=0,
+        )
+        picker = jnp.where(pages_c[:, unit : unit + 1] == key_l, 1.0, 0.0).astype(BF16)
+        picked = dot(picker, columns)
+        for x in range(4):
+            tile = picked[:, x * 128 : (x + 1) * 128].reshape(64, 2, 4, 128)
+            send_ref[:, x, 2 * unit : 2 * unit + 2, :, :] = tile.astype(BF16)
+        third = third_c[:, UNITS + unit : UNITS + unit + 1]
+        term = dot(jnp.where(third == key_l, 1.0, 0.0).astype(BF16), columns)
+        extra = term if unit == 0 else extra + term
+    for x in range(4):
+        tile = extra[:, x * 128 : (x + 1) * 128].reshape(64, 4, 128)
+        send_ref[:, x, 2 * UNITS, :, :] = tile.astype(BF16)
+
+    own = jnp.sum(jnp.where(row == group, table_f, 0.0), axis=0, keepdims=True)
+    for unit in range(UNITS):
+        info_ref[unit] = jnp.sum(jnp.where(col[:1] == unit, own, 0.0)).astype(jnp.int32)
+    info_ref[UNITS] = jnp.sum(jnp.where(col[:1] == 2 * UNITS, own, 0.0)).astype(jnp.int32)
+    info_ref[UNITS + 1] = jnp.sum(heavy[:1]).astype(jnp.int32)
+
+
+def label_kernel(info_ref, targets_ref, clips_ref, col_ref, row_ref):
+    targets = targets_ref[...]
+    clips = clips_ref[...] + 1
+    row, col = iota((128, 128), 0), iota((128, 128), 1)
+    earlier = jnp.where(row < col, 1.0, 0.0).astype(BF16)
+    ones = jnp.ones((128, 128), BF16)
+    for unit in range(UNITS):
+        arriving = targets == info_ref[unit]
+        rank = dot(jnp.where(arriving, 1.0, 0.0).astype(BF16), earlier).astype(jnp.int32)
+        for slot in range(3):
+            labels = jnp.where(arriving & (rank == slot), clips, 0).astype(F32).astype(BF16)
+            col_ref[unit, slot * SPAN : (slot + 1) * SPAN, :] = dot(labels, ones)
+            row_ref[unit, :, slot * SPAN : (slot + 1) * SPAN] = dot(ones[:8], labels, ROWS_T)
+
+
+def attend_unit(d_ref, e_ref, col_ref, row_ref, unit, count):
+    scale = HD**-0.5
+    start = pl.multiple_of(unit * (2 * SPAN), 2 * SPAN)
+    places = [start, start + SPAN] + ([2 * UNITS * SPAN] if count == 3 else [])
+
+    def load(a):
+        return jnp.concatenate([d_ref[a, pl.ds(place, SPAN), :] for place in places], axis=0)
+
+    key, value = load(1), load(2)
+    row_labels = row_ref[unit, 0:1, : count * SPAN]
+    grad_key, grad_value = None, None
+    for n, place in enumerate(places):
+        query = d_ref[0, pl.ds(place, SPAN), :]
+        cotangent = d_ref[3, pl.ds(place, SPAN), :]
+        labels = col_ref[unit, n * SPAN : (n + 1) * SPAN, :]
+        related = jnp.concatenate([labels] * (2 * count), axis=1) == row_labels
+        scores = jnp.where(related, dot(query, key, ROWS_T), -1e30)
+        top = jnp.max(scores, axis=1, keepdims=True)
+        weights = jnp.exp2((scores - top) * (scale * 1.4426950408889634))
+        probs = weights * (1.0 / jnp.sum(weights, axis=1, keepdims=True))
+        probs_b = probs.astype(BF16)
+        attended = dot(probs_b, value).astype(BF16)
+        delta = jnp.sum(cotangent.astype(F32) * attended.astype(F32), axis=1, keepdims=True)
+        dscores = (probs * (dot(cotangent, value, ROWS_T) - delta)).astype(BF16)
+        e_ref[0, pl.ds(place, SPAN), :] = attended
+        e_ref[1, pl.ds(place, SPAN), :] = (dot(dscores, key) * scale).astype(BF16)
+        term_key = dot(dscores, query, COLS_T)
+        term_value = dot(probs_b, cotangent, COLS_T)
+        grad_key = term_key if n == 0 else grad_key + term_key
+        grad_value = term_value if n == 0 else grad_value + term_value
+    for n, place in enumerate(places):
+        part = slice(n * SPAN, (n + 1) * SPAN)
+        e_ref[2, pl.ds(place, SPAN), :] = (grad_key[part] * scale).astype(BF16)
+        e_ref[3, pl.ds(place, SPAN), :] = grad_value[part].astype(BF16)
+
+
+def attend_kernel(info_ref, col_ref, row_ref, came_ref, out_ref, d_ref, e_ref):
+    row, col = iota((SPAN, SPAN), 0), iota((SPAN, SPAN), 1)
+    apart = jnp.where(((row & 31) << 3) + (row >> 5) == col, 1.0, 0.0).astype(BF16)
+    together = jnp.where(((col & 31) << 3) + (col >> 5) == row, 1.0, 0.0).astype(BF16)
+    apart_1 = jnp.where(((row & 63) << 2) + (row >> 6) == col, 1.0, 0.0).astype(BF16)
+    together_1 = jnp.where(((col & 63) << 2) + (col >> 6) == row, 1.0, 0.0).astype(BF16)
+    last = 2 * UNITS
+
+    def split(block, carry):
+        base = pl.multiple_of(block * 32, 32)
+        rows = jnp.concatenate(
+            [
+                came_ref[pl.ds(base, 32), 2 * j : 2 * j + 2, :, :].astype(F32).reshape(SPAN, 128)
+                for j in range(UNITS)
+            ],
+            axis=1,
+        ).astype(BF16)
+        parted = dot(apart, rows).astype(BF16)
+        for j in range(UNITS):
+            for i in range(2):
+                for a in range(4):
+                    at = (4 * i + a) * 32
+                    d_ref[a, pl.ds(pl.multiple_of((2 * j + i) * SPAN + base, 32), 32), :] = parted[
+                        at : at + 32, j * 128 : (j + 1) * 128
+                    ]
+        return carry
+
+    lax.fori_loop(0, 8, split, 0)
+    rows = jnp.concatenate(
+        [
+            came_ref[n * 64 : (n + 1) * 64, last, :, :].astype(F32).reshape(SPAN, 128)
+            for n in range(4)
+        ],
+        axis=1,
+    ).astype(BF16)
+    parted = dot(apart_1, rows).astype(BF16)
+    for n in range(4):
+        for a in range(4):
+            at = last * SPAN + n * 64
+            d_ref[a, at : at + 64, :] = parted[a * 64 : (a + 1) * 64, n * 128 : (n + 1) * 128]
+    for b in range(4):
+        e_ref[b, last * SPAN :, :] = jnp.zeros((SPAN, 128), BF16)
+
+    third = info_ref[UNITS]
+
+    def each_unit(unit, carry):
+        @pl.when(unit == third)
+        def _():
+            attend_unit(d_ref, e_ref, col_ref, row_ref, unit, 3)
+
+        @pl.when(unit != third)
+        def _():
+            attend_unit(d_ref, e_ref, col_ref, row_ref, unit, 2)
+
+        return carry
+
+    lax.fori_loop(0, UNITS, each_unit, 0)
+
+    def join(block, carry):
+        base = pl.multiple_of(block * 32, 32)
+        rows = jnp.concatenate(
+            [
+                jnp.concatenate(
+                    [
+                        e_ref[b, pl.ds(pl.multiple_of((2 * j + i) * SPAN + base, 32), 32), :]
+                        for i in range(2)
+                        for b in range(4)
+                    ],
+                    axis=0,
+                )
+                for j in range(UNITS)
+            ],
+            axis=1,
+        )
+        joined = dot(together, rows)
+        for j in range(UNITS):
+            tile = joined[:, j * 128 : (j + 1) * 128].reshape(32, 2, 4, 128)
+            out_ref[pl.ds(base, 32), 2 * j : 2 * j + 2, :, :] = tile.astype(BF16)
+        return carry
+
+    lax.fori_loop(0, 8, join, 0)
+    rows = jnp.concatenate(
+        [
+            jnp.concatenate(
+                [e_ref[b, last * SPAN + n * 64 : last * SPAN + (n + 1) * 64, :] for b in range(4)],
+                axis=0,
+            )
+            for n in range(4)
+        ],
+        axis=1,
+    )
+    joined = dot(together_1, rows)
+    for n in range(4):
+        tile = joined[:, n * 128 : (n + 1) * 128].reshape(64, 4, 128)
+        out_ref[n * 64 : (n + 1) * 64, last, :, :] = tile.astype(BF16)
+
+
+def home_kernel(codes_ref, thirds_ref, home_ref, back_ref, o_ref, dq_ref, dk_ref, dv_ref):
+    home = home_ref[...]
+    home_2 = jnp.concatenate([home] * 2, axis=1)
+    home_4 = jnp.concatenate([home] * 4, axis=1)
+    extra = jnp.concatenate(
+        [back_ref[:, x, 2 * UNITS, :, :].astype(F32).reshape(256, 128) for x in range(4)], axis=1
+    ).astype(BF16)
+    for unit in range(UNITS):
+        rows = jnp.concatenate(
+            [
+                back_ref[:, x, 2 * unit : 2 * unit + 2, :, :].astype(F32).reshape(512, 128)
+                for x in range(4)
+            ],
+            axis=1,
+        ).astype(BF16)
+        picker = jnp.where(home_4 == codes_ref[unit : unit + 1, :], 1.0, 0.0).astype(BF16)
+        third = jnp.where(home_2 == thirds_ref[unit : unit + 1, :], 1.0, 0.0).astype(BF16)
+        total = dot(picker, rows) + dot(third, extra)
+        for b, ref in enumerate((o_ref, dq_ref, dk_ref, dv_ref)):
+            for x in range(4):
+                at = (6 * x + unit) * HD
+                ref[:, at : at + HD] = total[
+                    b * 128 : (b + 1) * 128, x * 128 : (x + 1) * 128
+                ].astype(BF16)
+
+
+VMEM = pl.BlockSpec(memory_space=pltpu.VMEM)
+SMEM = pl.BlockSpec(memory_space=pltpu.SMEM)
+SHAPE = jax.ShapeDtypeStruct
+
+
+def kernel_params():
+    return pltpu.CompilerParams(vmem_limit_bytes=40 * MIB)
+
+
+def pack(me, targets, arrays):
+    return pl.pallas_call(
+        pack_kernel,
+        out_shape=(
+            SHAPE((64, 4, PAGES, 4, 128), BF16),
+            SHAPE((8, 512), F32),
+            SHAPE((8, 256), F32),
+            SHAPE((512, 128), F32),
+            SHAPE((8,), jnp.int32),
+        ),
+        in_specs=[SMEM] + [VMEM] * 5,
+        out_specs=(VMEM, VMEM, VMEM, VMEM, SMEM),
+        compiler_params=kernel_params(),
+    )(me, targets, *arrays)
+
+
+def label(info, targets, clips):
+    return pl.pallas_call(
+        label_kernel,
+        out_shape=(SHAPE((UNITS, 3 * SPAN, 128), F32), SHAPE((UNITS, 8, 3 * SPAN), F32)),
+        in_specs=[SMEM, VMEM, VMEM],
+        out_specs=(VMEM, VMEM),
+        compiler_params=kernel_params(),
+    )(info, targets, clips)
+
+
+def attend(info, col, row, came):
+    return pl.pallas_call(
+        attend_kernel,
+        out_shape=SHAPE((SPAN, PAGES, 4, 128), BF16),
+        in_specs=[SMEM, VMEM, VMEM, VMEM],
+        out_specs=VMEM,
+        scratch_shapes=[
+            pltpu.VMEM((4, PAGES * SPAN, 128), BF16),
+            pltpu.VMEM((4, PAGES * SPAN, 128), BF16),
+        ],
+        compiler_params=kernel_params(),
+    )(info, col, row, came)
+
+
+def unpack(codes, thirds, home, back):
+    return pl.pallas_call(
+        home_kernel,
+        out_shape=(SHAPE((128, 24 * HD), BF16),) * 4,
+        in_specs=[VMEM] * 4,
+        out_specs=(VMEM,) * 4,
+        compiler_params=kernel_params(),
+    )(codes, thirds, home, back)
+
+
+def body(queries, keys, values, upstream, dest_group, clip_ids):
+    group = lax.axis_index("dp")
+    device = group * 4 + lax.axis_index("seq")
+    targets = dest_group.reshape(SPAN, 128)
+    clips = clip_ids.reshape(SPAN, 128)
+    me = jnp.stack((device, group)).astype(jnp.int32)
+    arrays = (queries, keys, values, upstream)
+    send, codes, thirds, home, info = pack(me, targets, arrays)
+
+    def exchange(blocks):
+        return lax.all_to_all(blocks, ("dp", "seq"), split_axis=0, concat_axis=0, tiled=True)
+
+    def paged_path():
+        came = exchange(send.reshape(SPAN, PAGES, 4, 128))
+        col, row = label(info, targets, clips)
+        back = exchange(attend(info, col, row, came))
+        return tuple(unpack(codes, thirds, home, back.reshape(64, 4, PAGES, 4, 128)))
+
+    return lax.cond(
+        UNITS * info[UNITS + 1] <= 64,
+        paged_path,
+        lambda: plain_path(queries, keys, values, upstream, dest_group, clip_ids),
+    )
+
 
 def solution(mesh):
     return jax.shard_map(

time: 485 us -> 221 us (0.46); the launches traced: 476 us -> 221 us
  local copies, waits for them, and re-layouts: 130 us -> 5 us
  matrix products: 91.9 us -> 0 us
  Pallas kernels: 0 us -> 33 us
  blocking collectives: 116 us -> 87.8 us
  other arithmetic: 22.2 us -> 0.08 us
  waiting for transfers between devices: 97.6 us -> 77.6 us
    dot_general x38 -> x0, matrix products: 91.9 us -> none  [the longest x6 21.5 us: attend_forward(): jnp.dot(probs_b, value_head, preferred_element_type=jnp.float32)]
    slice x1, local copies, waits for them, and re-layouts: 35.7 us -> 1.2 us  [body(): info[UNITS + 1]]
    reshape x4 -> x0, local copies, waits for them, and re-layouts: 33.6 us -> none  [the longest x2 20.3 us: body(): blocks = packed.reshape(group_count, capacity, 4, part_count, width)]
    pallas_call x0 -> x4, Pallas kernels: none -> 33 us  [the longest x1 18.6 us: attend(): pl.pallas_call(attend_kernel, out_shape=SHAPE((SPAN, PAGES, 4, 128), BF16...]
    all_to_all x1, blocking collectives: 116 us -> 87.8 us  [exchange(): lax.all_to_all(blocks, ('dp', 'seq'), split_axis=0, concat_axis=0, tiled=...]
    unnamed x136 -> x10, local copies, waits for them, and re-layouts: 23 us -> 0.03 us
    all_to_all x1, waiting for transfers between devices: 97.6 us -> 77.6 us  [exchange(): lax.all_to_all(blocks, ('dp', 'seq'), split_axis=0, concat_axis=0, tiled=...]
    another operation x5 -> x0, local copies, waits for them, and re-layouts: 16.2 us -> none  [body(): jnp.stack((attended, gradients[0], gradients[1], gradients[2]), axis=1)]
  transfers between devices with their start and end apart: 1 -> 1, of which waited for: 1 -> 1; matrix products, arithmetic and copies ran while one was open for 2% -> 0% of each run, Pallas kernels for 0% -> 1%
where the time goes in v3:
time: 221 us
  blocking collectives  87.8 us (40%)
  waiting for transfers between devices  77.6 us (35%)
  Pallas kernels  33 us (15%)
  starting transfers between devices  15.6 us (7%)
  local copies, waits for them, and re-layouts  5 us (2%)
    all_to_all x1, blocking collectives, exchange(): lax.all_to_all(blocks, ('dp', 'seq'), split_axis=0, concat_axis=0, tiled=...  87.8 us
    all_to_all x1, waiting for transfers between devices, exchange(): lax.all_to_all(blocks, ('dp', 'seq'), split_axis=0, concat_axis=0, tiled=...  77.6 us
    pallas_call x1, Pallas kernels, attend(): pl.pallas_call(attend_kernel, out_shape=SHAPE((SPAN, PAGES, 4, 128), BF16...  18.6 us
    all_to_all x1, starting transfers between devices, exchange(): lax.all_to_all(blocks, ('dp', 'seq'), split_axis=0, concat_axis=0, tiled=...  15.6 us
    pallas_call x1, Pallas kernels, pack(): pl.pallas_call(pack_kernel, out_shape=(SHAPE((64, 4, PAGES, 4, 128), BF16...  7.69 us
  transfers between devices with their start and end apart: 1, of which 1 were waited for; matrix products, arithmetic and copies ran while one was open for 0% of the time, Pallas kernels for 1%

profile of v3, /device:TPU:1, one launch (start us, length us, event | category | flops | bytes accessed | tf_op | source)
XLA Modules:
  0.0 220.8 jit_solution(3645977344002892642)
XLA Ops:
  0.6 0.0 copy-start.10
  0.6 0.0 copy-start.27
  0.7 0.0 copy-start.28
  0.7 0.0 copy-start.29
  0.7 0.0 copy-start.30
  0.7 0.1 pad_add_fusion.me_ref
  0.8 7.7 %shard_map.101 = (bf16[64,4,13,4,128]{4,3,2,1,0:T(4,128)(2,1)}, f32[8,512]{1,0:T(8,128)}, f32[8,256]{1,0:T(8,128)}, f32[512,128]{1,0:T(8,128)}, s32[8]{0:T(128)}) custom-call(s32[2]{0:T(128)S(1)} %pad_add_fusion.me_ref, s32[256,128]{1,0:T(8,128)} %bitcast.63, bf16[128,3072]{1,0:T(8,128)(2,1)} %q_ref.1, bf16[128,3072]{1,0:T(8,128)(2,1)} %k_ref.1, ...), custom_call_target="tpu_custom_call" | custom-call | tf_op jit(solution)/shard_map/pallas_call | solution.py:480
  8.5 1.2 slice.124
  10.3 0.0 copy-done.10
  10.3 0.0 copy-done.27
  10.3 0.0 copy-done.28
  10.4 0.0 copy-done.29
  10.4 0.0 copy-done.30
  10.4 210.5 %conditional.1 = ((bf16[128,3072]{1,0:T(8,128)(2,1)}, bf16[128,3072]{1,0:T(8,128)(2,1)}, bf16[128,3072]{1,0:T(8,128)(2,1)}, bf16[128,3072]{1,0:T(8,128)(2,1)})) conditional(s32[]{:T(128)} %bitcast.26, (s32[32768,1]{0,1:T(1,128)S(1)}, s32[32768]{0:T(1024)}, bf16[128,3072]{1,0:T(8,128)(2,1)S(1)}, bf16[128,3072]{1,0:T(8,128)(2,1)S(1)}, ...), branch_computations={%region_0.22_spmd, %region_22.23_spmd} | conditional | flops 6839240704 | bytes 459571264 | solution.py:547
  10.6 0.0 copy-start.11
  10.6 0.6 copy-done.11
  11.3 15.6 %all-to-all-start = ((bf16[256,13,4,128]{3,2,1,0:T(4,128)(2,1)}), bf16[256,13,4,128]{3,2,1,0:T(4,128)(2,1)S(1)}, u32[]{:S(2)}, u32[]{:S(2)}) async-start(bf16[256,13,4,128]{3,2,1,0:T(4,128)(2,1)} %bitcast.62), calls=%async_computation | async-start | bytes 6815744 | tf_op jit(solution)/shard_map/cond/branch_1_fun/all_to_all | solution.py:539
  26.9 2.5 %branch_1_fun.3 = (f32[6,768,128]{2,1,0:T(8,128)S(1)}, f32[6,8,768]{2,1,0:T(8,128)S(1)}) custom-call(s32[8]{0:T(128)} %get-tuple-element.36.info_ref, s32[256,128]{1,0:T(8,128)} %copy-done.11, s32[256,128]{1,0:T(8,128)} %bitcast.73), custom_call_target="tpu_custom_call" | custom-call | tf_op jit(solution)/shard_map/cond/branch_1_fun/pallas_call | solution.py:496
  29.4 0.0 copy-start
  29.4 1.4 copy-done
  30.9 77.6 %all-to-all-done.came_ref = bf16[256,13,4,128]{3,2,1,0:T(4,128)(2,1)S(1)} async-done(((bf16[256,13,4,128]{3,2,1,0:T(4,128)(2,1)}), bf16[256,13,4,128]{3,2,1,0:T(4,128)(2,1)S(1)}, u32[]{:S(2)}, u32[]{:S(2)}) %all-to-all-start) | async-done | bytes 3407904 | tf_op jit(solution)/shard_map/cond/branch_1_fun/all_to_all | solution.py:539
  108.4 0.0 copy-start.1
  108.4 1.7 copy-done.1
  110.1 18.6 %branch_1_fun.4 = bf16[256,13,4,128]{3,2,1,0:T(4,128)(2,1)S(1)} custom-call(s32[8]{0:T(128)} %get-tuple-element.36.info_ref, f32[6,768,128]{2,1,0:T(8,128)S(1)} %copy-done.1, f32[6,8,768]{2,1,0:T(8,128)S(1)} %get-tuple-element.40.row_ref, bf16[256,13,4,128]{3,2,1,0:T(4,128)(2,1)S(1)} %all-to-all-done.came_ref), custom_call_target="tpu_custom_call" | custom-call | tf_op jit(solution)/shard_map/cond/branch_1_fun/pallas_call | solution.py:506
  128.7 0.0 copy-start.32
  128.7 0.0 copy-start.37
  128.7 0.0 copy-start.38
  128.8 87.8 %all_to_all.17 = bf16[256,13,4,128]{3,2,1,0:T(4,128)(2,1)S(1)} all-to-all(bf16[256,13,4,128]{3,2,1,0:T(4,128)(2,1)S(1)} %branch_1_fun.4), channel_id=1, replica_groups=mesh['dp'=64,'seq'=4] {'dp','seq'}, dimensions={0} | all-to-all | bytes 6815744 | tf_op jit(solution)/shard_map/cond/branch_1_fun/all_to_all | solution.py:539
  216.6 0.0 copy-done.32
  216.6 0.0 copy-done.37
  216.6 0.0 copy-done.38
  216.6 4.2 %branch_1_fun.5 = (bf16[128,3072]{1,0:T(8,128)(2,1)}, bf16[128,3072]{1,0:T(8,128)(2,1)}, bf16[128,3072]{1,0:T(8,128)(2,1)}, bf16[128,3072]{1,0:T(8,128)(2,1)}) custom-call(f32[8,512]{1,0:T(8,128)S(1)} %copy-done.37, f32[8,256]{1,0:T(8,128)S(1)} %copy-done.38, f32[512,128]{1,0:T(8,128)S(1)} %copy-done.32, bf16[64,4,13,4,128]{4,3,2,1,0:T(4,128)(2,1)S(1)} %bitcast.58), custom_call_target="tpu_custom_call" | custom-call | tf_op jit(solution)/shard_map/cond/branch_1_fun/pallas_call | solution.py:520
Async XLA Ops:
  0.6 9.7 %copy-start.10 = (s32[32768,1]{0,1:T(1,128)S(1)}, s32[32768,1]{0,1:T(1,128)}, u32[]{:S(2)}) copy-start(s32[32768,1]{0,1:T(1,128)} %param.12) | copy-start | bytes 393220
  0.6 9.7 %copy-start.27 = (bf16[128,3072]{1,0:T(8,128)(2,1)S(1)}, bf16[128,3072]{1,0:T(8,128)(2,1)}, u32[]{:S(2)}) copy-start(bf16[128,3072]{1,0:T(8,128)(2,1)} %q_ref.1) | copy-start | bytes 2359300
  0.7 9.7 %copy-start.28 = (bf16[128,3072]{1,0:T(8,128)(2,1)S(1)}, bf16[128,3072]{1,0:T(8,128)(2,1)}, u32[]{:S(2)}) copy-start(bf16[128,3072]{1,0:T(8,128)(2,1)} %k_ref.1) | copy-start | bytes 2359300
  0.7 9.7 %copy-start.29 = (bf16[128,3072]{1,0:T(8,128)(2,1)S(1)}, bf16[128,3072]{1,0:T(8,128)(2,1)}, u32[]{:S(2)}) copy-start(bf16[128,3072]{1,0:T(8,128)(2,1)} %v_ref.1) | copy-start | bytes 2359300
  0.7 9.7 %copy-start.30 = (bf16[128,3072]{1,0:T(8,128)(2,1)S(1)}, bf16[128,3072]{1,0:T(8,128)(2,1)}, u32[]{:S(2)}) copy-start(bf16[128,3072]{1,0:T(8,128)(2,1)} %u_ref.1) | copy-start | bytes 2359300
  10.6 0.7 copy-start.11
  11.3 97.2 %all-to-all-start = ((bf16[256,13,4,128]{3,2,1,0:T(4,128)(2,1)}), bf16[256,13,4,128]{3,2,1,0:T(4,128)(2,1)S(1)}, u32[]{:S(2)}, u32[]{:S(2)}) async-start(bf16[256,13,4,128]{3,2,1,0:T(4,128)(2,1)} %bitcast.62), calls=%async_computation | async-start | bytes 6815744 | tf_op jit(solution)/shard_map/cond/branch_1_fun/all_to_all | solution.py:539
  29.4 1.4 copy-start
  108.4 1.7 copy-start.1
  128.7 87.9 %copy-start.32 = (f32[512,128]{1,0:T(8,128)S(1)}, f32[512,128]{1,0:T(8,128)}, u32[]{:S(2)}) copy-start(f32[512,128]{1,0:T(8,128)} %get-tuple-element.35.home_ref) | copy-start | bytes 786436 | tf_op jit(solution)/shard_map/cond
  128.7 87.9 %copy-start.37 = (f32[8,512]{1,0:T(8,128)S(1)}, f32[8,512]{1,0:T(8,128)}, u32[]{:S(2)}) copy-start(f32[8,512]{1,0:T(8,128)} %get-tuple-element.33.codes_ref) | copy-start | bytes 49156 | tf_op jit(solution)/shard_map/cond
  128.7 87.9 %copy-start.38 = (f32[8,256]{1,0:T(8,128)S(1)}, f32[8,256]{1,0:T(8,128)}, u32[]{:S(2)}) copy-start(f32[8,256]{1,0:T(8,128)} %get-tuple-element.34.thirds_ref) | copy-start | bytes 24580 | tf_op jit(solution)/shard_map/cond

commit v4 on v3

--- a/solution.py
+++ b/solution.py
@@ -210,10 +210,24 @@
 
 
 def pack_kernel(
-    me_ref, targets_ref, q_ref, k_ref, v_ref, u_ref, send_ref, codes_ref, thirds_ref, home_ref, info_ref
+    me_ref,
+    targets_ref,
+    clips_ref,
+    q_ref,
+    k_ref,
+    v_ref,
+    u_ref,
+    send_ref,
+    codes_ref,
+    thirds_ref,
+    home_ref,
+    marks_ref,
+    info_ref,
+    heavies_ref,
 ):
     device, group = me_ref[0], me_ref[1]
     targets = targets_ref[...]
+    marks_ref[...] = 4 * targets + clips_ref[...] + 1
     lane = iota((SPAN, 128), 1)
     ones = jnp.ones((128, 128), BF16)
     flags = jnp.zeros((SPAN, 128), jnp.int32)
@@ -290,12 +304,12 @@
     for unit in range(UNITS):
         info_ref[unit] = jnp.sum(jnp.where(col[:1] == unit, own, 0.0)).astype(jnp.int32)
     info_ref[UNITS] = jnp.sum(jnp.where(col[:1] == 2 * UNITS, own, 0.0)).astype(jnp.int32)
-    info_ref[UNITS + 1] = jnp.sum(heavy[:1]).astype(jnp.int32)
-
-
-def label_kernel(info_ref, targets_ref, clips_ref, col_ref, row_ref):
-    targets = targets_ref[...]
-    clips = clips_ref[...] + 1
+    heavies_ref[0] = jnp.sum(heavy[:1]).astype(jnp.int32)
+
+
+def label_kernel(info_ref, marks_ref, row_ref):
+    targets = marks_ref[...] >> 2
+    clips = marks_ref[...] & 3
     row, col = iota((128, 128), 0), iota((128, 128), 1)
     earlier = jnp.where(row < col, 1.0, 0.0).astype(BF16)
     ones = jnp.ones((128, 128), BF16)
@@ -304,47 +318,53 @@
         rank = dot(jnp.where(arriving, 1.0, 0.0).astype(BF16), earlier).astype(jnp.int32)
         for slot in range(3):
             labels = jnp.where(arriving & (rank == slot), clips, 0).astype(F32).astype(BF16)
-            col_ref[unit, slot * SPAN : (slot + 1) * SPAN, :] = dot(labels, ones)
             row_ref[unit, :, slot * SPAN : (slot + 1) * SPAN] = dot(ones[:8], labels, ROWS_T)
 
 
-def attend_unit(d_ref, e_ref, col_ref, row_ref, unit, count):
+def attend_units(d_ref, e_ref, row_ref, units):
     scale = HD**-0.5
-    start = pl.multiple_of(unit * (2 * SPAN), 2 * SPAN)
-    places = [start, start + SPAN] + ([2 * UNITS * SPAN] if count == 3 else [])
-
-    def load(a):
-        return jnp.concatenate([d_ref[a, pl.ds(place, SPAN), :] for place in places], axis=0)
-
-    key, value = load(1), load(2)
-    row_labels = row_ref[unit, 0:1, : count * SPAN]
-    grad_key, grad_value = None, None
-    for n, place in enumerate(places):
-        query = d_ref[0, pl.ds(place, SPAN), :]
-        cotangent = d_ref[3, pl.ds(place, SPAN), :]
-        labels = col_ref[unit, n * SPAN : (n + 1) * SPAN, :]
-        related = jnp.concatenate([labels] * (2 * count), axis=1) == row_labels
-        scores = jnp.where(related, dot(query, key, ROWS_T), -1e30)
+    everything = []
+    for unit, count in units:
+        start = pl.multiple_of(unit * (2 * SPAN), 2 * SPAN)
+        spans = [(start, 2 * SPAN)] + ([(2 * UNITS * SPAN, SPAN)] if count == 3 else [])
+
+        def load(a, spans=spans):
+            parts = [d_ref[a, pl.ds(place, size), :] for place, size in spans]
+            return parts[0] if len(parts) == 1 else jnp.concatenate(parts, axis=0)
+
+        labels = row_ref[unit, :, : count * SPAN]
+        first = jnp.where(iota((8, 128), 0) == 0, 1.0, 0.0).astype(BF16)
+        column = dot(labels.astype(BF16), first, COLS_T)
+        related = jnp.concatenate([column] * (2 * count), axis=1) == labels[:1]
+        query, key, value, cotangent = load(0), load(1), load(2), load(3)
+        scores = dot(query, key, ROWS_T)
+        dprobs = dot(cotangent, value, ROWS_T)
+        everything.append([spans, query, key, value, cotangent, related, scores, dprobs])
+    for state in everything:
+        related, scores = state[5], state[6]
+        scores = jnp.where(related, scores, -1e30)
         top = jnp.max(scores, axis=1, keepdims=True)
         weights = jnp.exp2((scores - top) * (scale * 1.4426950408889634))
         probs = weights * (1.0 / jnp.sum(weights, axis=1, keepdims=True))
-        probs_b = probs.astype(BF16)
+        state += [probs, probs.astype(BF16)]
+    for spans, query, key, value, cotangent, related, scores, dprobs, probs, probs_b in everything:
         attended = dot(probs_b, value).astype(BF16)
         delta = jnp.sum(cotangent.astype(F32) * attended.astype(F32), axis=1, keepdims=True)
-        dscores = (probs * (dot(cotangent, value, ROWS_T) - delta)).astype(BF16)
-        e_ref[0, pl.ds(place, SPAN), :] = attended
-        e_ref[1, pl.ds(place, SPAN), :] = (dot(dscores, key) * scale).astype(BF16)
-        term_key = dot(dscores, query, COLS_T)
-        term_value = dot(probs_b, cotangent, COLS_T)
-        grad_key = term_key if n == 0 else grad_key + term_key
-        grad_value = term_value if n == 0 else grad_value + term_value
-    for n, place in enumerate(places):
-        part = slice(n * SPAN, (n + 1) * SPAN)
-        e_ref[2, pl.ds(place, SPAN), :] = (grad_key[part] * scale).astype(BF16)
-        e_ref[3, pl.ds(place, SPAN), :] = grad_value[part].astype(BF16)
-
-
-def attend_kernel(info_ref, col_ref, row_ref, came_ref, out_ref, d_ref, e_ref):
+        dscores = (probs * (dprobs - delta)).astype(BF16)
+        results = (
+            attended,
+            (dot(dscores, key) * scale).astype(BF16),
+            (dot(query, dscores, COLS_T) * scale).T.astype(BF16),
+            dot(cotangent, probs_b, COLS_T).T.astype(BF16),
+        )
+        for b, result in enumerate(results):
+            at = 0
+            for place, size in spans:
+                e_ref[b, pl.ds(place, size), :] = result[at : at + size]
+                at += size
+
+
+def attend_kernel(info_ref, row_ref, came_ref, out_ref, d_ref, e_ref):
     row, col = iota((SPAN, SPAN), 0), iota((SPAN, SPAN), 1)
     apart = jnp.where(((row & 31) << 3) + (row >> 5) == col, 1.0, 0.0).astype(BF16)
     together = jnp.where(((col & 31) << 3) + (col >> 5) == row, 1.0, 0.0).astype(BF16)
@@ -371,7 +391,7 @@
                     ]
         return carry
 
-    lax.fori_loop(0, 8, split, 0)
+    lax.fori_loop(0, 8, split, 0, unroll=8)
     rows = jnp.concatenate(
         [
             came_ref[n * 64 : (n + 1) * 64, last, :, :].astype(F32).reshape(SPAN, 128)
@@ -389,18 +409,18 @@
 
     third = info_ref[UNITS]
 
-    def each_unit(unit, carry):
-        @pl.when(unit == third)
+    def each_pair(pair, carry):
+        @pl.when(pair == third >> 1)
         def _():
-            attend_unit(d_ref, e_ref, col_ref, row_ref, unit, 3)
-
-        @pl.when(unit != third)
+            attend_units(d_ref, e_ref, row_ref, ((third, 3), (third ^ 1, 2)))
+
+        @pl.when(pair != third >> 1)
         def _():
-            attend_unit(d_ref, e_ref, col_ref, row_ref, unit, 2)
+            attend_units(d_ref, e_ref, row_ref, ((2 * pair, 2), (2 * pair + 1, 2)))
 
         return carry
 
-    lax.fori_loop(0, UNITS, each_unit, 0)
+    lax.fori_loop(0, UNITS // 2, each_pair, 0)
 
     def join(block, carry):
         base = pl.multiple_of(block * 32, 32)
@@ -424,7 +444,7 @@
             out_ref[pl.ds(base, 32), 2 * j : 2 * j + 2, :, :] = tile.astype(BF16)
         return carry
 
-    lax.fori_loop(0, 8, join, 0)
+    lax.fori_loop(0, 8, join, 0, unroll=8)
     rows = jnp.concatenate(
         [
             jnp.concatenate(
@@ -476,7 +496,7 @@
     return pltpu.CompilerParams(vmem_limit_bytes=40 * MIB)
 
 
-def pack(me, targets, arrays):
+def pack(me, targets, clips, arrays):
     return pl.pallas_call(
         pack_kernel,
         out_shape=(
@@ -484,36 +504,38 @@
             SHAPE((8, 512), F32),
             SHAPE((8, 256), F32),
             SHAPE((512, 128), F32),
+            SHAPE((SPAN, 128), jnp.int32),
             SHAPE((8,), jnp.int32),
+            SHAPE((1,), jnp.int32),
         ),
-        in_specs=[SMEM] + [VMEM] * 5,
-        out_specs=(VMEM, VMEM, VMEM, VMEM, SMEM),
+        in_specs=[SMEM] + [VMEM] * 6,
+        out_specs=(VMEM,) * 5 + (SMEM, SMEM),
         compiler_params=kernel_params(),
-    )(me, targets, *arrays)
-
-
-def label(info, targets, clips):
+    )(me, targets, clips, *arrays)
+
+
+def label(info, marks):
     return pl.pallas_call(
         label_kernel,
-        out_shape=(SHAPE((UNITS, 3 * SPAN, 128), F32), SHAPE((UNITS, 8, 3 * SPAN), F32)),
-        in_specs=[SMEM, VMEM, VMEM],
-        out_specs=(VMEM, VMEM),
+        out_shape=SHAPE((UNITS, 8, 3 * SPAN), F32),
+        in_specs=[SMEM, VMEM],
+        out_specs=VMEM,
         compiler_params=kernel_params(),
-    )(info, targets, clips)
-
-
-def attend(info, col, row, came):
+    )(info, marks)
+
+
+def attend(info, row, came):
     return pl.pallas_call(
         attend_kernel,
         out_shape=SHAPE((SPAN, PAGES, 4, 128), BF16),
-        in_specs=[SMEM, VMEM, VMEM, VMEM],
+        in_specs=[SMEM, VMEM, VMEM],
         out_specs=VMEM,
         scratch_shapes=[
             pltpu.VMEM((4, PAGES * SPAN, 128), BF16),
             pltpu.VMEM((4, PAGES * SPAN, 128), BF16),
         ],
         compiler_params=kernel_params(),
-    )(info, col, row, came)
+    )(info, row, came)
 
 
 def unpack(codes, thirds, home, back):
@@ -533,19 +555,18 @@
     clips = clip_ids.reshape(SPAN, 128)
     me = jnp.stack((device, group)).astype(jnp.int32)
     arrays = (queries, keys, values, upstream)
-    send, codes, thirds, home, info = pack(me, targets, arrays)
+    send, codes, thirds, home, marks, info, heavies = pack(me, targets, clips, arrays)
 
     def exchange(blocks):
         return lax.all_to_all(blocks, ("dp", "seq"), split_axis=0, concat_axis=0, tiled=True)
 
     def paged_path():
         came = exchange(send.reshape(SPAN, PAGES, 4, 128))
-        col, row = label(info, targets, clips)
-        back = exchange(attend(info, col, row, came))
+        back = exchange(attend(info, label(info, marks), came))
         return tuple(unpack(codes, thirds, home, back.reshape(64, 4, PAGES, 4, 128)))
 
     return lax.cond(
-        UNITS * info[UNITS + 1] <= 64,
+        UNITS * heavies.reshape(()) <= 64,
         paged_path,
         lambda: plain_path(queries, keys, values, upstream, dest_group, clip_ids),
     )

time: 221 us -> 210 us (0.950)
  Pallas kernels: 33 us -> 25.2 us
  local copies, waits for them, and re-layouts: 5 us -> 0.05 us
    pallas_call x1, Pallas kernels: 18.6 us -> 11 us  [attend(): pl.pallas_call(attend_kernel, out_shape=SHAPE((SPAN, PAGES, 4, 128), BF16...]
    cond x12 -> x6, local copies, waits for them, and re-layouts: 3.77 us -> 0.01 us
where the time goes in v4:
time: 210 us
  blocking collectives  87.8 us (42%)
  waiting for transfers between devices  79.3 us (38%)
  Pallas kernels  25.2 us (12%)
  starting transfers between devices  15.7 us (7%)
    all_to_all x1, blocking collectives, exchange(): lax.all_to_all(blocks, ('dp', 'seq'), split_axis=0, concat_axis=0, tiled=...  87.8 us
    all_to_all x1, waiting for transfers between devices, exchange(): lax.all_to_all(blocks, ('dp', 'seq'), split_axis=0, concat_axis=0, tiled=...  79.3 us
    all_to_all x1, starting transfers between devices, exchange(): lax.all_to_all(blocks, ('dp', 'seq'), split_axis=0, concat_axis=0, tiled=...  15.7 us
    pallas_call x1, Pallas kernels, attend(): pl.pallas_call(attend_kernel, out_shape=SHAPE((SPAN, PAGES, 4, 128), BF16...  11 us
    pallas_call x1, Pallas kernels, pack(): pl.pallas_call(pack_kernel, out_shape=(SHAPE((64, 4, PAGES, 4, 128), BF16...  7.73 us
    pallas_call x1, Pallas kernels, unpack(): pl.pallas_call(home_kernel, out_shape=(SHAPE((128, 24 * HD), BF16),) * 4,...  4.23 us
  transfers between devices with their start and end apart: 1, of which 1 were waited for; matrix products, arithmetic and copies ran while one was open for 0% of the time, Pallas kernels for 1%

profile of v4, /device:TPU:1, one launch (start us, length us, event | category | flops | bytes accessed | tf_op | source)
XLA Modules:
  0.0 209.8 jit_solution(468343548634763474)
XLA Ops:
  0.6 0.0 copy-start.14
  0.6 0.0 copy-start.28
  0.7 0.0 copy-start.24
  0.7 0.0 copy-start.25
  0.7 0.0 copy-start.26
  0.7 0.0 copy-start.27
  0.7 0.1 pad_add_fusion.me_ref
  0.8 7.7 %shard_map.101 = (bf16[64,4,13,4,128]{4,3,2,1,0:T(4,128)(2,1)}, f32[8,512]{1,0:T(8,128)}, f32[8,256]{1,0:T(8,128)}, f32[512,128]{1,0:T(8,128)}, s32[256,128]{1,0:T(8,128)}, /*index=5*/s32[8]{0:T(128)}, s32[1]{0:T(128)}) custom-call(s32[2]{0:T(128)S(1)} %pad_add_fusion.me_ref, s32[256,128]{1,0:T(8,128)} %bitcast.63, s32[256,128]{1,0:T(8,128)} %bitcast.72, ...), custom_call_target="tpu_custom_call" | custom-call | tf_op jit(solution)/shard_map/pallas_call | solution.py:500
  9.2 0.0 copy-done.14
  9.2 0.0 copy-done.28
  9.2 0.0 copy-done.24
  9.2 0.0 copy-done.25
  9.2 0.0 copy-done.26
  9.2 0.0 copy-done.27
  9.2 200.6 %conditional.1 = ((bf16[128,3072]{1,0:T(8,128)(2,1)}, bf16[128,3072]{1,0:T(8,128)(2,1)}, bf16[128,3072]{1,0:T(8,128)(2,1)}, bf16[128,3072]{1,0:T(8,128)(2,1)})) conditional(s32[]{:T(128)} %bitcast.26, (s32[32768,1]{0,1:T(1,128)S(1)}, s32[32768]{0:T(1024)S(1)}, bf16[128,3072]{1,0:T(8,128)(2,1)S(1)}, bf16[128,3072]{1,0:T(8,128)(2,1)S(1)}, ...), branch_computations={%region_0.22_spmd, %region_22.23_spmd} | conditional | flops 6839240704 | bytes 459046944 | solution.py:568
  9.5 15.7 %all-to-all-start = ((bf16[256,13,4,128]{3,2,1,0:T(4,128)(2,1)}), bf16[256,13,4,128]{3,2,1,0:T(4,128)(2,1)S(1)}, u32[]{:S(2)}, u32[]{:S(2)}) async-start(bf16[256,13,4,128]{3,2,1,0:T(4,128)(2,1)} %bitcast.62), calls=%async_computation | async-start | bytes 6815744 | tf_op jit(solution)/shard_map/cond/branch_1_fun/all_to_all | solution.py:561
  25.1 2.2 %branch_1_fun.3.row_ref = f32[6,8,768]{2,1,0:T(8,128)S(1)} custom-call(s32[8]{0:T(128)} %get-tuple-element.33.info_ref, s32[256,128]{1,0:T(8,128)} %get-tuple-element.34.marks_ref), custom_call_target="tpu_custom_call" | custom-call | tf_op jit(solution)/shard_map/cond/branch_1_fun/pallas_call | solution.py:518
  27.3 79.3 %all-to-all-done.came_ref = bf16[256,13,4,128]{3,2,1,0:T(4,128)(2,1)S(1)} async-done(((bf16[256,13,4,128]{3,2,1,0:T(4,128)(2,1)}), bf16[256,13,4,128]{3,2,1,0:T(4,128)(2,1)S(1)}, u32[]{:S(2)}, u32[]{:S(2)}) %all-to-all-start) | async-done | bytes 3407904 | tf_op jit(solution)/shard_map/cond/branch_1_fun/all_to_all | solution.py:561
  106.7 11.0 %branch_1_fun.4 = bf16[256,13,4,128]{3,2,1,0:T(4,128)(2,1)S(1)} custom-call(s32[8]{0:T(128)} %get-tuple-element.33.info_ref, f32[6,8,768]{2,1,0:T(8,128)S(1)} %branch_1_fun.3.row_ref, bf16[256,13,4,128]{3,2,1,0:T(4,128)(2,1)S(1)} %all-to-all-done.came_ref), custom_call_target="tpu_custom_call" | custom-call | tf_op jit(solution)/shard_map/cond/branch_1_fun/pallas_call | solution.py:528
  117.7 0.0 copy-start.29
  117.7 0.0 copy-start.34
  117.7 0.0 copy-start.35
  117.7 87.8 %all_to_all.17 = bf16[256,13,4,128]{3,2,1,0:T(4,128)(2,1)S(1)} all-to-all(bf16[256,13,4,128]{3,2,1,0:T(4,128)(2,1)S(1)} %branch_1_fun.4), channel_id=1, replica_groups=mesh['dp'=64,'seq'=4] {'dp','seq'}, dimensions={0} | all-to-all | bytes 6815744 | tf_op jit(solution)/shard_map/cond/branch_1_fun/all_to_all | solution.py:561
  205.6 0.0 copy-done.29
  205.6 0.0 copy-done.34
  205.6 0.0 copy-done.35
  205.6 4.2 %branch_1_fun.5 = (bf16[128,3072]{1,0:T(8,128)(2,1)}, bf16[128,3072]{1,0:T(8,128)(2,1)}, bf16[128,3072]{1,0:T(8,128)(2,1)}, bf16[128,3072]{1,0:T(8,128)(2,1)}) custom-call(f32[8,512]{1,0:T(8,128)S(1)} %copy-done.34, f32[8,256]{1,0:T(8,128)S(1)} %copy-done.35, f32[512,128]{1,0:T(8,128)S(1)} %copy-done.29, bf16[64,4,13,4,128]{4,3,2,1,0:T(4,128)(2,1)S(1)} %bitcast.58), custom_call_target="tpu_custom_call" | custom-call | tf_op jit(solution)/shard_map/cond/branch_1_fun/pallas_call | solution.py:542
Async XLA Ops:
  0.6 8.5 %copy-start.14 = (s32[32768,1]{0,1:T(1,128)S(1)}, s32[32768,1]{0,1:T(1,128)}, u32[]{:S(2)}) copy-start(s32[32768,1]{0,1:T(1,128)} %param.12) | copy-start | bytes 393220
  0.6 8.5 %copy-start.28 = (s32[32768]{0:T(1024)S(1)}, s32[32768]{0:T(1024)}, u32[]{:S(2)}) copy-start(s32[32768]{0:T(1024)} %param.13) | copy-start | bytes 393220
  0.7 8.5 %copy-start.24 = (bf16[128,3072]{1,0:T(8,128)(2,1)S(1)}, bf16[128,3072]{1,0:T(8,128)(2,1)}, u32[]{:S(2)}) copy-start(bf16[128,3072]{1,0:T(8,128)(2,1)} %q_ref.1) | copy-start | bytes 2359300
  0.7 8.5 %copy-start.25 = (bf16[128,3072]{1,0:T(8,128)(2,1)S(1)}, bf16[128,3072]{1,0:T(8,128)(2,1)}, u32[]{:S(2)}) copy-start(bf16[128,3072]{1,0:T(8,128)(2,1)} %k_ref.1) | copy-start | bytes 2359300
  0.7 8.5 %copy-start.26 = (bf16[128,3072]{1,0:T(8,128)(2,1)S(1)}, bf16[128,3072]{1,0:T(8,128)(2,1)}, u32[]{:S(2)}) copy-start(bf16[128,3072]{1,0:T(8,128)(2,1)} %v_ref.1) | copy-start | bytes 2359300
  0.7 8.5 %copy-start.27 = (bf16[128,3072]{1,0:T(8,128)(2,1)S(1)}, bf16[128,3072]{1,0:T(8,128)(2,1)}, u32[]{:S(2)}) copy-start(bf16[128,3072]{1,0:T(8,128)(2,1)} %u_ref.1) | copy-start | bytes 2359300
  9.5 97.2 %all-to-all-start = ((bf16[256,13,4,128]{3,2,1,0:T(4,128)(2,1)}), bf16[256,13,4,128]{3,2,1,0:T(4,128)(2,1)S(1)}, u32[]{:S(2)}, u32[]{:S(2)}) async-start(bf16[256,13,4,128]{3,2,1,0:T(4,128)(2,1)} %bitcast.62), calls=%async_computation | async-start | bytes 6815744 | tf_op jit(solution)/shard_map/cond/branch_1_fun/all_to_all | solution.py:561
  117.7 87.9 %copy-start.29 = (f32[512,128]{1,0:T(8,128)S(1)}, f32[512,128]{1,0:T(8,128)}, u32[]{:S(2)}) copy-start(f32[512,128]{1,0:T(8,128)} %get-tuple-element.32.home_ref) | copy-start | bytes 786436 | tf_op jit(solution)/shard_map/cond
  117.7 87.9 %copy-start.34 = (f32[8,512]{1,0:T(8,128)S(1)}, f32[8,512]{1,0:T(8,128)}, u32[]{:S(2)}) copy-start(f32[8,512]{1,0:T(8,128)} %get-tuple-element.30.codes_ref) | copy-start | bytes 49156 | tf_op jit(solution)/shard_map/cond
  117.7 87.9 %copy-start.35 = (f32[8,256]{1,0:T(8,128)S(1)}, f32[8,256]{1,0:T(8,128)}, u32[]{:S(2)}) copy-start(f32[8,256]{1,0:T(8,128)} %get-tuple-element.31.thirds_ref) | copy-start | bytes 24580 | tf_op jit(solution)/shard_map/cond
